TPU v7x, 32 devices: a whole 2x2x4 slice. The times are simulated.
32 devices in a mesh: dp: 4 (over x, core), tensor: 8 (over z, y).
Axes of the slice: x: 2, y: 2, z: 4, core: 2. Of those that a mesh axis runs over, the one named last changes fastest.
Arguments:
- tokens: bfloat16 [16384, 1024], P(('dp', 'tensor')), may hold values from -6 to 6
- lengths: int32 [8], P('dp'), may hold values from 1 to 2048, as said below
- ln1_gain: float32 [1024], replicated, may hold values from 0.5 to 1.5
- ln1_bias: float32 [1024], replicated, may hold values from -3 to 3
- w_query: bfloat16 [1024, 1024], P(None, 'tensor'), may hold values from -0.1875 to 0.1875
- w_key: bfloat16 [1024, 1024], P(None, 'tensor'), may hold values from -0.1875 to 0.1875
- w_value: bfloat16 [1024, 1024], P(None, 'tensor'), may hold values from -0.1875 to 0.1875
- w_out: bfloat16 [1024, 1024], P('tensor'), may hold values from -1.5 to 1.5
- ln2_gain: float32 [1024], replicated, may hold values from 0.5 to 1.5
- ln2_bias: float32 [1024], replicated, may hold values from -3 to 3
- w_gate: bfloat16 [1024, 4096], P(None, 'tensor'), may hold values from -0.1875 to 0.1875
- w_up: bfloat16 [1024, 4096], P(None, 'tensor'), may hold values from -0.1875 to 0.1875
- w_down: bfloat16 [4096, 1024], P('tensor'), may hold values from -0.09375 to 0.09375
- cotangent: bfloat16 [16384, 1024], P(('dp', 'tensor')), may hold values from -6 to 6
Outputs:
- output: bfloat16 [16384, 1024], P(('dp', 'tensor'))
- grad_tokens: bfloat16 [16384, 1024], P(('dp', 'tensor'))
- grad_ln1_gain: float32 [1024], replicated
- grad_ln1_bias: float32 [1024], replicated
- grad_w_query: float32 [1024, 1024], P(None, 'tensor')
- grad_w_key: float32 [1024, 1024], P(None, 'tensor')
- grad_w_value: float32 [1024, 1024], P(None, 'tensor')
- grad_w_out: float32 [1024, 1024], P('tensor')
- grad_ln2_gain: float32 [1024], replicated
- grad_ln2_bias: float32 [1024], replicated
- grad_w_gate: float32 [1024, 4096], P(None, 'tensor')
- grad_w_up: float32 [1024, 4096], P(None, 'tensor')
- grad_w_down: float32 [4096, 1024], P('tensor')
Inputs may be any that keep to these rules, and one draw needn't show every extreme that they name: `lengths`: slot w holds the rows w * 2048 to w * 2048 + 2047; rows of a slot past its length are padding. Among the 2 slots of each index of dp, one holds exactly 2048 live rows.
All inputs are finite; a program needn't handle non-finite values.
Results may differ from a plain program's by a relative error of at most 0.024.
Values may be sent and summed in bfloat16 or wider, within the bound.
A program may use at most 320 MiB of HBM per device.

v0:
```python
import jax
import jax.numpy as jnp
from jax import lax
from jax.sharding import PartitionSpec as P

HD = 64
WIN = 2048


EPSILON = 1e-05
LAST_DIMS = (((1,), (1,)), ((), ()))
FIRST_DIMS = (((0,), (0,)), ((), ()))


def rope_tables():
    half_width = HD // 2
    frequency = 10000.0 ** (-jnp.arange(half_width, dtype=jnp.float32) * 2.0 / HD)
    angles = jnp.arange(WIN, dtype=jnp.float32)[:, None] * frequency[None, :]
    angles = jnp.concatenate([angles, angles], axis=1)
    return (jnp.cos(angles), jnp.sin(angles))


def rotate_pairs(values_in, cosines, sines):
    half_width = values_in.shape[-1] // 2
    swapped = jnp.concatenate([-values_in[..., half_width:], values_in[..., :half_width]], axis=-1)
    return values_in * cosines + swapped * sines


def norm_forward(values_in, norm_gain, norm_bias):
    centre = values_in - jnp.mean(values_in, axis=-1, keepdims=True)
    inverse = lax.rsqrt(jnp.mean(centre * centre, axis=-1, keepdims=True) + EPSILON)
    scaled = centre * inverse
    return (scaled * norm_gain + norm_bias, scaled, inverse)


def norm_backward(grad_in, scaled, inverse, norm_gain):
    weighted = grad_in * norm_gain
    first_mean = jnp.mean(weighted, axis=-1, keepdims=True)
    second_mean = jnp.mean(weighted * scaled, axis=-1, keepdims=True)
    grad_rows = inverse * (weighted - first_mean - scaled * second_mean)
    return (grad_rows, jnp.sum(grad_in * scaled, axis=0), jnp.sum(grad_in, axis=0))


def attend_forward(queries, keys_all, values_all, lengths):
    slot_count = queries.shape[0]
    head_count = queries.shape[2]
    block_rows = min(512, WIN)
    block_count = WIN // block_rows
    score_scale = HD ** (-0.5)
    query_blocks = queries.reshape(slot_count * block_count, block_rows, head_count, HD)
    slot_ids = jnp.arange(slot_count * block_count, dtype=jnp.int32) // block_count
    positions = jnp.arange(WIN, dtype=jnp.int32)

    def attend_one_block(block_item):
        query_block, slot_id = block_item
        key_slot = keys_all[slot_id]
        value_slot = values_all[slot_id]
        live_keys = positions < lengths[slot_id]
        scores = (
            jnp.einsum("qhd,khd->hqk", query_block, key_slot, preferred_element_type=jnp.float32)
            * score_scale
        )
        scores = jnp.where(live_keys[None, None, :], scores, -1e30)
        row_max = jnp.max(scores, axis=2, keepdims=True)
        shifted = jnp.exp(scores - row_max)
        denom_sum = jnp.sum(shifted, axis=2, keepdims=True)
        attn_probs = (shifted / denom_sum).astype(jnp.bfloat16)
        block_mixed = jnp.einsum(
            "hqk,khd->qhd", attn_probs, value_slot, preferred_element_type=jnp.float32
        )
        return (block_mixed, (row_max + jnp.log(denom_sum))[:, :, 0])

    mixed, log_norm = lax.map(attend_one_block, (query_blocks, slot_ids))
    return (
        mixed.reshape(slot_count, WIN, head_count, HD),
        log_norm.reshape(slot_count, block_count, head_count, block_rows),
    )


def attend_backward(queries, keys_all, values_all, grad_mixed, log_norm, lengths):
    slot_count = queries.shape[0]
    head_count = queries.shape[2]
    block_rows = min(512, WIN)
    block_count = WIN // block_rows
    score_scale = HD ** (-0.5)
    positions = jnp.arange(WIN, dtype=jnp.int32)

    def one_slot(slot_item):
        query_slot, grad_slot, norm_slot, slot_length, key_slot, value_slot = slot_item
        live_keys = (positions < slot_length)[None, None, :]

        def one_one_block(carry, block_item):
            grad_keys, grad_values = carry
            query_block, grad_block, norm_block = block_item
            scores = (
                jnp.einsum(
                    "qhd,khd->hqk", query_block, key_slot, preferred_element_type=jnp.float32
                )
                * score_scale
            )
            attn_probs = jnp.where(live_keys, jnp.exp(scores - norm_block[:, :, None]), 0.0)
            grad_probs = jnp.einsum(
                "qhd,khd->hqk", grad_block, value_slot, preferred_element_type=jnp.float32
            )
            row_dot = jnp.sum(attn_probs * grad_probs, axis=2, keepdims=True)
            grad_scores = (attn_probs * (grad_probs - row_dot) * score_scale).astype(jnp.bfloat16)
            grad_query = jnp.einsum(
                "hqk,khd->qhd", grad_scores, key_slot, preferred_element_type=jnp.float32
            )
            grad_keys = grad_keys + jnp.einsum(
                "hqk,qhd->khd", grad_scores, query_block, preferred_element_type=jnp.float32
            )
            grad_values = grad_values + jnp.einsum(
                "hqk,qhd->khd",
                attn_probs.astype(jnp.bfloat16),
                grad_block,
                preferred_element_type=jnp.float32,
            )
            return ((grad_keys, grad_values), grad_query)

        zeros_slot = jnp.zeros((WIN, head_count, HD), jnp.float32)
        (grad_keys, grad_values), grad_query = lax.scan(
            one_one_block, (zeros_slot, zeros_slot), (query_slot, grad_slot, norm_slot)
        )
        return (grad_query.reshape(WIN, head_count, HD), grad_keys, grad_values)

    block_shape = (slot_count, block_count, block_rows, head_count, HD)
    return lax.map(
        one_slot,
        (
            queries.reshape(block_shape),
            grad_mixed.reshape(block_shape),
            log_norm,
            lengths,
            keys_all,
            values_all,
        ),
    )


def per_device(
    tokens,
    lengths,
    ln1_gain,
    ln1_bias,
    w_query,
    w_key,
    w_value,
    w_out,
    ln2_gain,
    ln2_bias,
    w_gate,
    w_up,
    w_down,
    cotangent,
):
    row_count = tokens.shape[0]
    own_start = lax.axis_index("tensor") * row_count
    slot_count = lengths.shape[0]
    all_rows = slot_count * WIN
    head_count = w_query.shape[1] // HD
    local_width = head_count * HD
    cosines, sines = rope_tables()
    cos_four = cosines[None, :, None, :]
    sin_four = sines[None, :, None, :]
    every_tokens = lax.all_gather(tokens, "tensor", axis=0, tiled=True).astype(jnp.float32)
    every_normed, every_scaled, every_inverse = norm_forward(every_tokens, ln1_gain, ln1_bias)
    normed_one = every_normed.astype(jnp.bfloat16)
    scaled_one = lax.dynamic_slice_in_dim(every_scaled, own_start, row_count, 0)
    inverse_one = lax.dynamic_slice_in_dim(every_inverse, own_start, row_count, 0)

    def head_rows(weight):
        return jnp.dot(normed_one, weight, preferred_element_type=jnp.float32).reshape(
            slot_count, WIN, head_count, HD
        )

    queries = rotate_pairs(head_rows(w_query), cos_four, sin_four).astype(jnp.bfloat16)
    keys_all = rotate_pairs(head_rows(w_key), cos_four, sin_four).astype(jnp.bfloat16)
    values_all = head_rows(w_value).astype(jnp.bfloat16)
    mixed, log_norm = attend_forward(queries, keys_all, values_all, lengths)
    mixed_low = mixed.reshape(all_rows, local_width).astype(jnp.bfloat16)
    attn_branch = lax.psum(
        jnp.dot(mixed_low, w_out, preferred_element_type=jnp.float32).astype(jnp.bfloat16), "tensor"
    ).astype(jnp.float32)
    middle = every_tokens + attn_branch
    every_two, scaled_two, inverse_two = norm_forward(middle, ln2_gain, ln2_bias)
    normed_two = every_two.astype(jnp.bfloat16)
    own_middle = lax.dynamic_slice_in_dim(middle, own_start, row_count, 0)
    gate_value = jnp.dot(normed_two, w_gate, preferred_element_type=jnp.float32)
    up_value = jnp.dot(normed_two, w_up, preferred_element_type=jnp.float32)
    sigmoid_gate = jax.nn.sigmoid(gate_value)
    silu_gate = gate_value * sigmoid_gate
    hidden = (silu_gate * up_value).astype(jnp.bfloat16)
    output = (
        own_middle
        + lax.psum_scatter(
            jnp.dot(hidden, w_down, preferred_element_type=jnp.float32).astype(jnp.bfloat16),
            "tensor",
            scatter_dimension=0,
            tiled=True,
        ).astype(jnp.float32)
    ).astype(jnp.bfloat16)
    every_seed = lax.all_gather(cotangent, "tensor", axis=0, tiled=True)
    grad_hidden = lax.dot_general(every_seed, w_down, LAST_DIMS, preferred_element_type=jnp.float32)
    grad_w_down = lax.dot_general(
        hidden, every_seed, FIRST_DIMS, preferred_element_type=jnp.float32
    )
    grad_gate = (
        grad_hidden * up_value * sigmoid_gate * (1.0 + gate_value * (1.0 - sigmoid_gate))
    ).astype(jnp.bfloat16)
    grad_up = (grad_hidden * silu_gate).astype(jnp.bfloat16)
    grad_w_gate = lax.dot_general(
        normed_two, grad_gate, FIRST_DIMS, preferred_element_type=jnp.float32
    )
    grad_w_up = lax.dot_general(normed_two, grad_up, FIRST_DIMS, preferred_element_type=jnp.float32)
    grad_normed_two = lax.psum(
        (
            lax.dot_general(grad_gate, w_gate, LAST_DIMS, preferred_element_type=jnp.float32)
            + lax.dot_general(grad_up, w_up, LAST_DIMS, preferred_element_type=jnp.float32)
        ).astype(jnp.bfloat16),
        "tensor",
    ).astype(jnp.float32)
    back_two, unused_gain, unused_bias = norm_backward(
        grad_normed_two, scaled_two, inverse_two, ln2_gain
    )
    grad_middle = every_seed.astype(jnp.float32) + back_two
    grad_middle_low = grad_middle.astype(jnp.bfloat16)
    own_grad_middle = lax.dynamic_slice_in_dim(grad_middle, own_start, row_count, 0)
    own_grad_two = lax.dynamic_slice_in_dim(grad_normed_two, own_start, row_count, 0)
    own_scaled_two = lax.dynamic_slice_in_dim(scaled_two, own_start, row_count, 0)
    gain_two_grad = jnp.sum(own_grad_two * own_scaled_two, axis=0)
    bias_two_grad = jnp.sum(own_grad_two, axis=0)
    grad_w_out = lax.dot_general(
        mixed_low, grad_middle_low, FIRST_DIMS, preferred_element_type=jnp.float32
    )
    grad_mixed = lax.dot_general(
        grad_middle_low, w_out, LAST_DIMS, preferred_element_type=jnp.float32
    ).astype(jnp.bfloat16)
    grad_mixed = grad_mixed.reshape(slot_count, WIN, head_count, HD)
    grad_query, grad_keys, grad_values = attend_backward(
        queries, keys_all, values_all, grad_mixed, log_norm, lengths
    )
    grad_query = (
        rotate_pairs(grad_query, cos_four, -sin_four)
        .reshape(all_rows, local_width)
        .astype(jnp.bfloat16)
    )
    grad_keys = (
        rotate_pairs(grad_keys, cos_four, -sin_four)
        .reshape(all_rows, local_width)
        .astype(jnp.bfloat16)
    )
    grad_values = grad_values.reshape(all_rows, local_width).astype(jnp.bfloat16)
    grad_w_query = lax.dot_general(
        normed_one, grad_query, FIRST_DIMS, preferred_element_type=jnp.float32
    )
    grad_w_key = lax.dot_general(
        normed_one, grad_keys, FIRST_DIMS, preferred_element_type=jnp.float32
    )
    grad_w_value = lax.dot_general(
        normed_one, grad_values, FIRST_DIMS, preferred_element_type=jnp.float32
    )
    summed = lax.dot_general(grad_query, w_query, LAST_DIMS, preferred_element_type=jnp.float32)
    summed = summed + lax.dot_general(
        grad_keys, w_key, LAST_DIMS, preferred_element_type=jnp.float32
    )
    grad_normed_one = lax.psum_scatter(
        (
            summed
            + lax.dot_general(grad_values, w_value, LAST_DIMS, preferred_element_type=jnp.float32)
        ).astype(jnp.bfloat16),
        "tensor",
        scatter_dimension=0,
        tiled=True,
    ).astype(jnp.float32)
    back_one, gain_one_grad, bias_one_grad = norm_backward(
        grad_normed_one, scaled_one, inverse_one, ln1_gain
    )
    grad_tokens = (own_grad_middle + back_one).astype(jnp.bfloat16)
    summed_weights = (
        lax.psum(grad_w_query.astype(jnp.bfloat16), "dp").astype(jnp.float32),
        lax.psum(grad_w_key.astype(jnp.bfloat16), "dp").astype(jnp.float32),
        lax.psum(grad_w_value.astype(jnp.bfloat16), "dp").astype(jnp.float32),
        lax.psum(grad_w_out.astype(jnp.bfloat16), "dp").astype(jnp.float32),
        lax.psum(grad_w_gate.astype(jnp.bfloat16), "dp").astype(jnp.float32),
        lax.psum(grad_w_up.astype(jnp.bfloat16), "dp").astype(jnp.float32),
        lax.psum(grad_w_down.astype(jnp.bfloat16), "dp").astype(jnp.float32),
    )
    summed_norms = lax.psum(
        (gain_one_grad, bias_one_grad, gain_two_grad, bias_two_grad), ("dp", "tensor")
    )
    return (
        output,
        grad_tokens,
        summed_norms[0],
        summed_norms[1],
        summed_weights[0],
        summed_weights[1],
        summed_weights[2],
        summed_weights[3],
        summed_norms[2],
        summed_norms[3],
        summed_weights[4],
        summed_weights[5],
        summed_weights[6],
    )


def solution(mesh):
    placed = (
        P(("dp", "tensor"), None),
        P("dp"),
        P(),
        P(),
        P(None, "tensor"),
        P(None, "tensor"),
        P(None, "tensor"),
        P("tensor", None),
        P(),
        P(),
        P(None, "tensor"),
        P(None, "tensor"),
        P("tensor", None),
        P(("dp", "tensor"), None),
    )
    return jax.shard_map(
        per_device,
        mesh=mesh,
        in_specs=placed,
        out_specs=(
            P(("dp", "tensor"), None),
            P(("dp", "tensor"), None),
            P(),
            P(),
            P(None, "tensor"),
            P(None, "tensor"),
            P(None, "tensor"),
            P("tensor", None),
            P(),
            P(),
            P(None, "tensor"),
            P(None, "tensor"),
            P("tensor", None),
        ),
        check_vma=False,
    )
```

profile of v0, /device:TPU:0, one launch (start us, length us, event | category | flops | bytes accessed | tf_op | source)
XLA Modules:
  0.0 1971.6 jit_solution(6486106486104480105)
XLA Ops:
  16.8 121.0 %all-gather.3.cloned.1.call-done = bf16[4096,1024]{1,0:T(8,128)(2,1)} async-done(((bf16[512,1024]{1,0:T(8,128)(2,1)}), bf16[4096,1024]{1,0:T(8,128)(2,1)}) %all-gather.3.cloned.1.call-update) | async-done | bytes 8388624 | tf_op jit(solution)/shard_map/all_gather | solution.py:166
  210.1 93.9 %while.44 = (s32[]{:T(128)}, bf16[8,512,2,64]{1,3,2,0:T(8,128)(2,1)}, f32[8,2,512]{2,1,0:T(2,128)}, s32[8]{0:T(128)S(1)}, bf16[2,2048,2,64]{1,3,2,0:T(8,128)(2,1...) while((s32[]{:T(128)}, ...), condition=%wide.region_5.6_spmd.clone, body=%wide.region_2.5_spmd.clone.sunk | while | flops 562037760 | bytes 30843108 | solution.py:73
  314.1 268.0 %all-reduce.6.cloned.1.call-done = bf16[4096,1024]{1,0:T(8,128)(2,1)} async-done(((bf16[4096,1024]{1,0:T(8,128)(2,1)}), bf16[4096,1024]{1,0:T(8,128)(2,1)}) %all-reduce.6.cloned.1.call-update) | async-done | bytes 8388624 | tf_op jit(solution)/shard_map/psum | solution.py:182
  626.9 81.3 %all-gather.5.cloned.1.call-done = bf16[4096,1024]{1,0:T(8,128)(2,1)} async-done(((bf16[512,1024]{1,0:T(8,128)(2,1)}), bf16[4096,1024]{1,0:T(8,128)(2,1)}) %all-gather.5.cloned.1.call-update) | async-done | bytes 8388624 | tf_op jit(solution)/shard_map/all_gather | solution.py:203
  782.4 230.3 %all-reduce.8.cloned.1.call-done = bf16[4096,1024]{1,0:T(8,128)(2,1)} async-done(((bf16[4096,1024]{1,0:T(8,128)(2,1)}), bf16[4096,1024]{1,0:T(8,128)(2,1)}) %all-reduce.8.cloned.1.call-update) | async-done | bytes 8388624 | tf_op jit(solution)/shard_map/psum | solution.py:216
  1050.4 453.4 %while.46 = (s32[]{:T(128)}, f32[2,2048,2,64]{1,0,3,2:T(2,128)}, f32[2,2048,2,64]{1,0,3,2:T(2,128)}, bf16[2,2048,2,64]{1,3,2,0:T(8,128)(2,1)}, bf16[2,4,512,2,64...) while((s32[]{:T(128)}, f32[2,2048,2,64]{1,0,3,2:T(2,128)}, ...), condition=%wide.region_17.18_spmd.clone, body=%wide.region_13.17_spmd.clone.sunk | while | flops 1397760000 | bytes 158679600 | solution.py:128
  1055.6 174.2 %while.47 = (s32[]{:T(128)}, f32[2048,2,64]{0,2,1:T(8,128)}, f32[2048,2,64]{0,2,1:T(8,128)}, f32[4,512,2,64]{1,3,2,0:T(8,128)}, bf16[4,512,2,64]{1,3,2,0:T(8,128...) while((s32[]{:T(128)}, f32[2048,2,64]{0,2,1:T(8,128)}, ...), condition=%wide.region_16.16_spmd.clone, body=%wide.region_14.15_spmd.clone.sunk | while | flops 1397757952 | bytes 140814608 | solution.py:122
  1082.5 16.4 fusion.214
  1126.2 16.4 fusion.214
  1169.8 16.4 fusion.214
  1213.4 16.4 fusion.214
  1232.1 18.4 dynamic_update_slice.42
  1258.6 18.4 dynamic_update_slice.41
  1282.0 174.2 %while.47 = (s32[]{:T(128)}, f32[2048,2,64]{0,2,1:T(8,128)}, f32[2048,2,64]{0,2,1:T(8,128)}, f32[4,512,2,64]{1,3,2,0:T(8,128)}, bf16[4,512,2,64]{1,3,2,0:T(8,128...) while((s32[]{:T(128)}, f32[2048,2,64]{0,2,1:T(8,128)}, ...), condition=%wide.region_16.16_spmd.clone, body=%wide.region_14.15_spmd.clone.sunk | while | flops 1397757952 | bytes 140814608 | solution.py:122
  1309.0 16.4 fusion.214
  1352.6 16.4 fusion.214
  1396.2 16.4 fusion.214
  1439.9 16.4 fusion.214
  1458.5 18.4 dynamic_update_slice.42
  1485.1 18.4 dynamic_update_slice.41
  1585.2 28.4 %all-reduce.10.cloned.1.call-done = (bf16[1024,128]{1,0:T(8,128)(2,1)}, bf16[1024,128]{1,0:T(8,128)(2,1)}, bf16[1024,128]{1,0:T(8,128)(2,1)}, bf16[128,1024]{1,0...) async-done(((bf16[1024,128]{1,0:T(8,128)(2,1)}, bf16[1024,128]{1,0:T(8,128)(2,1)}, bf16[1024,128]{1,0:T(8,128)(2,1)}, ...) | async-done | bytes 4194320 | tf_op jit(solution)/shard_map/psum | solution.py:281
  1628.1 138.7 %reduce-scatter.3.cloned.1.call-done = bf16[512,1024]{1,0:T(8,128)(2,1)} async-done(((bf16[4096,1024]{1,0:T(8,128)(2,1)}), bf16[512,1024]{1,0:T(8,128)(2,1)}) %reduce-scatter.3.cloned.1.call-update) | async-done | bytes 1048592 | tf_op jit(solution)/shard_map/reduce_scatter | solution.py:196
  1770.0 148.5 %reduce-scatter.5.cloned.1.call-done = bf16[512,1024]{1,0:T(8,128)(2,1)} async-done(((bf16[4096,1024]{1,0:T(8,128)(2,1)}), bf16[512,1024]{1,0:T(8,128)(2,1)}) %reduce-scatter.5.cloned.1.call-update) | async-done | bytes 1048592 | tf_op jit(solution)/shard_map/reduce_scatter | solution.py:267
  1921.1 39.4 %all-reduce = (f32[1024]{0:T(1024)}, f32[1024]{0:T(1024)}, f32[1024]{0:T(1024)}, f32[1024]{0:T(1024)}) all-reduce(f32[1024]{0:T(1024)S(1)} %get-tuple-element.301, f32[1024]{0:T(1024)S(1)} %get-tuple-element.308, f32[1024]{0:T(1024)S(1)} %get-tuple-element.304, ...), channel_id=1, replica_groups=mesh['dp'=4,'tensor'=8] {'dp','tensor'}, use_global_device_ids=true, to_apply=%region_22.23 | all-reduce | flops 4096 | bytes 32768 | tf_op jit(solution)/shard_map/psum | solution.py:289
  (403 shorter events, 679.9 us)
Async XLA Ops:
  7.2 701.0 %copy-start = (bf16[512,1024]{1,0:T(8,128)(2,1)S(1)}, bf16[512,1024]{1,0:T(8,128)(2,1)}, u32[]{:S(2)}) copy-start(bf16[512,1024]{1,0:T(8,128)(2,1)} %param.32) | copy-start | bytes 3145732
  7.2 130.6 %all-gather.3.cloned.1.call-start = ((), (), s32[]{:S(2)}) async-start(), calls=%async_computation.2 | async-start | bytes 9437184 | tf_op jit(solution)/shard_map/all_gather | solution.py:166
  7.9 574.1 %all-reduce.6.cloned.1.call-start = ((), (), s32[]{:S(2)}) async-start(), calls=%async_computation.3 | async-start | bytes 16777216 | tf_op jit(solution)/shard_map/psum | solution.py:182
  11.2 135.2 %copy-start.16 = (f32[2048,64]{0,1:T(8,128)}, f32[2048,64]{0,1:T(8,128)S(1)}, u32[]{:S(2)}) copy-start(f32[2048,64]{0,1:T(8,128)S(1)} %get-tuple-element.403) | copy-start | bytes 1572868
  16.8 129.6 %copy-start.35 = (f32[1024]{0:T(1024)S(1)}, f32[1024]{0:T(1024)}, u32[]{:S(2)}) copy-start(f32[1024]{0:T(1024)} %param.22) | copy-start | bytes 12292
  16.8 129.6 %copy-start.39 = (f32[1024]{0:T(1024)S(1)}, f32[1024]{0:T(1024)}, u32[]{:S(2)}) copy-start(f32[1024]{0:T(1024)} %param.23) | copy-start | bytes 12292
  156.6 10.9 copy-start.26
  173.8 15.7 copy-start.7
  179.5 14.8 copy-start.24
  210.1 97.5 %copy-start.29 = (bf16[128,1024]{1,0:T(8,128)(2,1)S(1)}, bf16[128,1024]{1,0:T(8,128)(2,1)}, u32[]{:S(2)}) copy-start(bf16[128,1024]{1,0:T(8,128)(2,1)} %param.27) | copy-start | bytes 786436
  313.3 394.9 %all-gather.5.cloned.1.call-start = ((), (), s32[]{:S(2)}) async-start(), calls=%async_computation.5 | async-start | bytes 9437184 | tf_op jit(solution)/shard_map/all_gather | solution.py:203
  314.0 698.6 %all-reduce.8.cloned.1.call-start = ((), (), s32[]{:S(2)}) async-start(), calls=%async_computation.6 | async-start | bytes 16777216 | tf_op jit(solution)/shard_map/psum | solution.py:216
  582.1 13.8 copy-start.5
  602.1 11.1 copy-start.43
  743.9 869.7 %all-reduce.10.cloned.1.call-start = ((), (), s32[]{:S(2)}) async-start(), calls=%async_computation.8 | async-start | bytes 8388608 | tf_op jit(solution)/shard_map/psum | solution.py:281
  756.5 14.7 slice-start.2
  1012.7 10.7 copy-start.6
  1023.4 10.4 copy-start.14
  1039.7 10.7 copy-start.33
  1039.7 10.7 copy-start.45
  1527.8 239.0 %reduce-scatter.3.cloned.1.call-start = ((), (), s32[]{:S(2)}) async-start(), calls=%async_computation.4 | async-start | bytes 9437184 | tf_op jit(solution)/shard_map/reduce_scatter | solution.py:196
  1536.8 381.6 %reduce-scatter.5.cloned.1.call-start = ((), (), s32[]{:S(2)}) async-start(), calls=%async_computation.7 | async-start | bytes 9437184 | tf_op jit(solution)/shard_map/reduce_scatter | solution.py:267
  1613.6 12.9 copy-start.28
  1613.6 304.9 %copy-start.36 = (f32[1024]{0:T(1024)S(1)}, f32[1024]{0:T(1024)}, u32[]{:S(2)}) copy-start(f32[1024]{0:T(1024)} %param.22) | copy-start | bytes 12292
  (64 other events, 313.3 us)
Sparse Core Ops, SparseCore 0:
  10.2 127.6 all-gather.2
  313.4 268.5 all-reduce.5
  584.2 123.9 all-gather.4
  744.1 268.5 all-reduce.7
  1527.9 85.6 all-reduce.9
  1617.5 149.2 reduce-scatter.2
  1770.4 148.0 reduce-scatter.4
where the time goes:
time: 1990 us; the launch traced here: 1970 us
  waiting for transfers between devices  1020 us (51%)
  matrix products  511 us (26%)
  local copies, waits for them, and re-layouts  210 us (11%)
  other arithmetic  162 us (8%)
  blocking collectives  39.4 us (2%)
    psum x1, waiting for transfers between devices, per_device(): lax.psum(jnp.dot(mixed_low, w_out, preferred_element_type=jnp.float32).as...  268 us
    psum x1, waiting for transfers between devices, per_device(): lax.psum((lax.dot_general(grad_gate, w_gate, LAST_DIMS, preferred_element...  230 us
    reduce_scatter x1, waiting for transfers between devices, per_device(): lax.psum_scatter((summed + lax.dot_general(grad_values, w_value, LAST_DIM...  148 us
    reduce_scatter x1, waiting for transfers between devices, per_device(): lax.psum_scatter(jnp.dot(hidden, w_down, preferred_element_type=jnp.float...  139 us
    dot_general x8, matrix products, one_one_block(): jnp.einsum('hqk,khd->qhd', grad_scores, key_slot, preferred_element_type=...  131 us
    all_gather x1, waiting for transfers between devices, per_device(): lax.all_gather(tokens, 'tensor', axis=0, tiled=True).astype(jnp.float32)  121 us
    dot_general x8, matrix products, one_one_block(): jnp.einsum('hqk,qhd->khd', grad_scores, query_block, preferred_element_ty...  121 us
    dynamic_update_slice x10, local copies, waits for them, and re-layouts, attend_backward(): lax.map(one_slot, (queries.reshape(block_shape), grad_mixed.reshape(block...  89.2 us
  transfers between devices with their start and end apart: 7, of which 7 were waited for; matrix products, arithmetic and copies ran while one was open for 8% of the time, Pallas kernels for 0%

commit v1 on v0

v1 whole, which is shorter than its diff:
```python
import functools

import jax
import jax.numpy as jnp
import numpy as np
from jax import lax
from jax.experimental import pallas as pl
from jax.experimental.pallas import tpu as pltpu
from jax.sharding import PartitionSpec as P

HD = 64
WIN = 2048
EPSILON = 1e-05
SCALE = HD ** (-0.5)
LOG2E = 1.4426950408889634
C2 = SCALE * LOG2E
NT = (((1,), (1,)), ((), ()))
NN = (((1,), (0,)), ((), ()))
TN = (((0,), (0,)), ((), ()))
MESH = pl.DeviceIdType.MESH
F32 = jnp.float32
BF16 = jnp.bfloat16
MIB = 1024 * 1024
HBM = pl.BlockSpec(memory_space=pl.ANY)
VMEM = pl.BlockSpec(memory_space=pltpu.VMEM)


def dot(a, b, dims=NN):
    return lax.dot_general(a, b, dims, preferred_element_type=F32)


def shape(dims, kind=BF16):
    return jax.ShapeDtypeStruct(dims, kind)


class Sizes:
    def __init__(self, n_dp, n_t, rows, d, cw, cfull):
        self.n_dp, self.n_t, self.rows, self.d = n_dp, n_t, rows, d
        self.X, self.H = n_dp // 2, n_t // 2
        self.G = WIN // rows
        self.NG = n_t // self.G
        self.cw, self.hw = cw, self.NG * cw
        self.cf = cfull // 2


class Place:
    def __init__(self, z):
        self.z = z
        dp, t = lax.axis_index("dp"), lax.axis_index("tensor")
        self.dp, self.t = dp, t
        self.x, self.c = dp // 2, dp % 2
        self.hi, self.lo = t // 2, t % 2
        self.g, self.r = t // z.G, t % z.G

    def core(self):
        return (self.x * 2 + 1 - self.c, self.t)

    def y(self):
        return (self.dp, self.hi * 2 + 1 - self.lo)

    def xi(self, i):
        return (self.x + i) % self.z.X

    def xdev(self, i):
        return (self.xi(i) * 2 + self.c, self.t)

    def hii(self, i):
        return (self.hi + i) % self.z.H

    def hdev(self, i):
        return (self.dp, self.hii(i) * 2 + self.lo)

    def ri(self, i):
        return (self.r + i) % self.z.G

    def rdev(self, i):
        return (self.dp, self.g * self.z.G + self.ri(i))

    def gi(self, i):
        return (self.g + i) % self.z.NG

    def gdev(self, i):
        return (self.dp, self.gi(i) * self.z.G + self.r)


class Net:
    def __init__(self, send, recv, local=None):
        self.send, self.recv, self.local_sem = send, recv, local
        self.count, self.local_count = 0, 0
        self.all = []

    def remote(self, src, dst, device):
        k = self.count
        self.count += 1
        cp = pltpu.make_async_remote_copy(
            src_ref=src, dst_ref=dst, send_sem=self.send.at[k], recv_sem=self.recv.at[k],
            device_id=device, device_id_type=MESH,
        )
        self.all.append(cp)
        return cp

    def local(self, src, dst):
        k = self.local_count
        self.local_count += 1
        return pltpu.make_async_copy(src, dst, self.local_sem.at[k])

    def wait_sends(self):
        for cp in self.all:
            cp.wait_send()


def meet(devices):
    barrier = pltpu.get_barrier_semaphore()
    for device in devices:
        pl.semaphore_signal(barrier, inc=1, device_id=device, device_id_type=MESH)
    pl.semaphore_wait(barrier, len(devices))


def part(i, n):
    return pl.ds(pl.multiple_of(i * n, n), n)


def comm_call(body, z, name, cid, out_shape, in_specs, out_specs, scratch=(), n=64, vmem=None):
    return pl.pallas_call(
        functools.partial(body, z),
        out_shape=out_shape,
        in_specs=in_specs,
        out_specs=out_specs,
        scratch_shapes=[
            pltpu.SemaphoreType.DMA((n,)),
            pltpu.SemaphoreType.DMA((n,)),
            pltpu.SemaphoreType.DMA((16,)),
            *scratch,
        ],
        compiler_params=pltpu.CompilerParams(
            collective_id=cid, has_side_effects=True, vmem_limit_bytes=vmem
        ),
        name=name,
    )


def gather_rows_kernel(z, n1, w3, n1s, w3s, send, recv, lsem):
    p, net = Place(z), Net(send, recv, lsem)
    rq = z.d // z.n_dp
    meet(
        [p.rdev(i) for i in range(1, z.G)]
        + [p.gdev(i) for i in range(1, z.NG)]
        + [p.xdev(i) for i in range(1, z.X)]
        + [p.core()]
    )
    mine = n1s.at[part(p.r, z.rows)]
    rows_out = [net.remote(n1, mine, p.rdev(i)) for i in range(1, z.G)]
    quarter = part(p.dp, rq)
    w_own = w3s.at[p.g, :, quarter]
    w_out = [net.remote(w3.at[:, quarter], w_own, p.gdev(i)) for i in range(1, z.NG)]
    for cp in w_out + rows_out:
        cp.start()
    keep = [net.local(n1, mine), net.local(w3.at[:, quarter], w_own)]
    for cp in keep:
        cp.start()
    keep[1].wait()
    for cp in w_out:
        cp.wait_recv()
    block = w3s.at[:, :, quarter]
    along = [net.remote(block, block, p.xdev(i)) for i in range(1, z.X)]
    for cp in along:
        cp.start()
    for cp in along:
        cp.wait_recv()
    across = []
    for x in range(z.X):
        block = w3s.at[:, :, part(x * 2 + p.c, rq)]
        across.append(net.remote(block, block, p.core()))
        across[-1].start()
    for cp in across + rows_out:
        cp.wait_recv()
    keep[0].wait()
    net.wait_sends()


def gather_weights_kernel(z, wo, wg, wu, wd, wos, wgs, wus, wds, send, recv, lsem):
    p, net = Place(z), Net(send, recv, lsem)
    qc = z.d // z.n_dp
    rx, dx, cf = z.d // z.X, z.cf // z.X, z.cf
    meet(
        [p.hdev(i) for i in range(1, z.H)]
        + [p.xdev(i) for i in range(1, z.X)]
        + [p.y(), p.core()]
    )

    def wo_rows(t):
        return part((t % z.G) * z.NG + t // z.G, z.cw)

    cols = part(p.dp, qc)
    own = wos.at[wo_rows(p.t), cols]
    o_out = [net.remote(wo.at[:, cols], own, p.hdev(i)) for i in range(1, z.H)]
    o_keep = net.local(wo.at[:, cols], own)
    o_keep.start()
    for cp in o_out:
        cp.start()

    def pieces(hi, x):
        return (
            wgs.at[part(x, rx), part(hi, cf)],
            wus.at[part(x, rx), part(hi, cf)],
            wds.at[pl.ds(pl.multiple_of(hi * cf + x * dx, 16), dx)],
        )

    src = (
        wg.at[part(p.x, rx), part(p.c, cf)],
        wu.at[part(p.x, rx), part(p.c, cf)],
        wd.at[pl.ds(pl.multiple_of(p.c * cf + p.x * dx, 16), dx)],
    )
    f_out = []
    for i in range(1, z.H):
        f_out.append([net.remote(a, b, p.hdev(i)) for a, b in zip(src, pieces(p.hi, p.x))])
        for cp in f_out[-1]:
            cp.start()
    keep = [
        net.local(wg.at[:, part(p.c, cf)], wgs.at[:, part(p.hi, cf)]),
        net.local(wu.at[:, part(p.c, cf)], wus.at[:, part(p.hi, cf)]),
        net.local(wd.at[part(p.c, cf)], wds.at[part(p.hi, cf)]),
    ]
    for cp in keep:
        cp.start()
    o_keep.wait()
    hop = [net.remote(own, own, p.y())]
    hop[0].start()
    for i in range(1, z.H):
        o_out[i - 1].wait_recv()
        block = wos.at[wo_rows(((p.hi + z.H - i) % z.H) * 2 + p.lo), cols]
        hop.append(net.remote(block, block, p.y()))
        hop[-1].start()
    f_hop = []
    for i in range(1, z.H):
        for cp in f_out[i - 1]:
            cp.wait_recv()
        for ref in pieces((p.hi + z.H - i) % z.H, p.x):
            for k in range(1, z.X):
                f_hop.append(net.remote(ref, ref, p.xdev(k)))
                f_hop[-1].start()
    for cp in hop:
        cp.wait_recv()
    along = []
    for k in range(1, z.X):
        block = wos.at[:, cols]
        along.append(net.remote(block, block, p.xdev(k)))
        along[-1].start()
    for cp in along:
        cp.wait_recv()
    across = []
    for x in range(z.X):
        block = wos.at[:, part(x * 2 + p.c, qc)]
        across.append(net.remote(block, block, p.core()))
        across[-1].start()
    for cp in f_hop + across:
        cp.wait_recv()
    for cp in keep:
        cp.wait()
    net.wait_sends()


def gather_four_kernel(z, own, four, send, recv, lsem):
    p, net = Place(z), Net(send, recv, lsem)
    meet([p.y(), p.core()])
    mine = four.at[p.lo * 2 + p.c]
    a = net.remote(own, mine, p.y())
    b = net.remote(own, mine, p.core())
    a.start()
    b.start()
    keep = net.local(own, mine)
    keep.start()
    a.wait_recv()
    other = four.at[(1 - p.lo) * 2 + p.c]
    e = net.remote(other, other, p.core())
    e.start()
    b.wait_recv()
    e.wait_recv()
    keep.wait()
    net.wait_sends()


def scatter_four_kernel(z, one, two, out_one, out_two, send, recv, lsem, rc, ry, sums):
    p, net = Place(z), Net(send, recv, lsem)
    meet([p.y(), p.core()])
    arrays = (two, one)
    outs = (out_two, out_one)
    first = []
    for k, ref in enumerate(arrays):
        pair = []
        for far in range(2):
            lo = p.lo if far == 0 else 1 - p.lo
            pair.append(net.remote(ref.at[lo * 2 + 1 - p.c], rc.at[k, far], p.core()))
        first.append(pair)
    for pair in first:
        pair[1].start()
        pair[0].start()
    second = []
    for k, ref in enumerate(arrays):
        first[k][1].wait_recv()
        total = ref[(1 - p.lo) * 2 + p.c].astype(F32) + rc[k, 1].astype(F32)
        sums[k] = total.astype(BF16)
        second.append(net.remote(sums.at[k], ry.at[k], p.y()))
        second[-1].start()
    for k, ref in enumerate(arrays):
        first[k][0].wait_recv()
        outs[k][...] = ref[p.lo * 2 + p.c].astype(F32) + rc[k, 0].astype(F32)
    for k in range(2):
        second[k].wait_recv()
        outs[k][...] = outs[k][...] + ry[k].astype(F32)
    net.wait_sends()


def mixed_kernel(z, mixed, own, send, recv, lsem):
    p, net = Place(z), Net(send, recv, lsem)
    meet([p.rdev(i) for i in range(1, z.G)])
    mine = own.at[:, part(p.r, z.hw)]
    out = [net.remote(mixed.at[part(p.ri(i), z.rows)], mine, p.rdev(i)) for i in range(1, z.G)]
    for cp in out:
        cp.start()
    keep = net.local(mixed.at[part(p.r, z.rows)], mine)
    keep.start()
    for cp in out:
        cp.wait_recv()
    keep.wait()
    net.wait_sends()


def unmix_kernel(z, own, every, send, recv, lsem):
    p, net = Place(z), Net(send, recv, lsem)
    meet([p.rdev(i) for i in range(1, z.G)])
    mine = every.at[part(p.r, z.rows)]
    out = [net.remote(own.at[:, part(p.ri(i), z.hw)], mine, p.rdev(i)) for i in range(1, z.G)]
    for cp in out:
        cp.start()
    keep = net.local(own.at[:, part(p.r, z.hw)], mine)
    keep.start()
    for cp in out:
        cp.wait_recv()
    keep.wait()
    net.wait_sends()


def scatter_rows_kernel(z, partial, got, send, recv, lsem):
    p, net = Place(z), Net(send, recv, lsem)
    meet([p.rdev(i) for i in range(1, z.G)])
    out = [net.remote(partial.at[p.ri(i)], got.at[i - 1], p.rdev(i)) for i in range(1, z.G)]
    for cp in out:
        cp.start()
    keep = net.local(partial.at[p.r], got.at[z.G - 1])
    keep.start()
    for cp in out:
        cp.wait_recv()
    keep.wait()
    net.wait_sends()


def add_refs(*values):
    total = values[0].astype(F32)
    for v in values[1:]:
        total = total + v.astype(F32)
    return total


def reduce_ffn_kernel(
    z, dg, du, dd, og, ou, od, send, recv, lsem, rgx, rux, rdx, sg, su, sd, rgz, ruz, rdz
):
    p, net = Place(z), Net(send, recv, lsem)
    rx, dx, cf = z.d // z.X, z.cf // z.X, z.cf
    meet([p.hdev(i) for i in range(1, z.H)] + [p.xdev(i) for i in range(1, z.X)] + [p.core()])
    first = []
    for i in range(1, z.X):
        xi = p.xi(i)
        first.append(
            (
                net.remote(dd.at[:, part(xi, dx)], rdx.at[i - 1], p.xdev(i)),
                net.remote(dg.at[part(xi, rx)], rgx.at[i - 1], p.xdev(i)),
                net.remote(du.at[part(xi, rx)], rux.at[i - 1], p.xdev(i)),
            )
        )
    for k in range(3):
        for trio in first:
            trio[k].start()
    seconds = []
    for k in range(3):
        for trio in first:
            trio[k].wait_recv()
        if k == 0:
            for h in range(z.H):
                sd[h] = add_refs(
                    dd[h, part(p.x, dx)], *[rdx[i, h] for i in range(z.X - 1)]
                ).astype(BF16)
        else:
            own, got, out = ((dg, rgx, sg), (du, rux, su))[k - 1]
            out[...] = add_refs(own[part(p.x, rx)], *[got[i] for i in range(z.X - 1)]).astype(BF16)
        group = []
        for i in range(1, z.H):
            hi = p.hii(i)
            if k == 0:
                group.append(net.remote(sd.at[hi], rdz.at[i - 1], p.hdev(i)))
            else:
                out, got = ((sg, rgz), (su, ruz))[k - 1]
                group.append(net.remote(out.at[:, part(hi, cf)], got.at[i - 1], p.hdev(i)))
            group[-1].start()
        seconds.append(group)
    thirds = []
    for k in range(3):
        for cp in seconds[k]:
            cp.wait_recv()
        if k == 0:
            at = pl.ds(pl.multiple_of(p.c * cf + p.x * dx, 16), dx)
            od[at] = add_refs(sd[p.hi], *[rdz[i] for i in range(z.H - 1)]).astype(BF16)
            block = od.at[at]
        else:
            part_sum, got, out = ((sg, rgz, og), (su, ruz, ou))[k - 1]
            out[part(p.x, rx), part(p.c, cf)] = add_refs(
                part_sum[:, part(p.hi, cf)], *[got[i] for i in range(z.H - 1)]
            ).astype(BF16)
            block = out.at[part(p.x, rx), part(p.c, cf)]
        group = [net.remote(block, block, p.xdev(i)) for i in range(1, z.X)]
        for cp in group:
            cp.start()
        thirds.append(group)
    last = []
    for k in range(3):
        for cp in thirds[k]:
            cp.wait_recv()
        if k == 0:
            block = od.at[part(p.c, cf)]
        else:
            block = (og, ou)[k - 1].at[:, part(p.c, cf)]
        last.append(net.remote(block, block, p.core()))
        last[-1].start()
    for cp in last:
        cp.wait_recv()
    net.wait_sends()


def reduce_attn_kernel(
    z, dw, do, ow, oo, send, recv, lsem, wc, wx, ws, wg, oc, ox, os_, oy, oy_sum, oz
):
    p, net = Place(z), Net(send, recv, lsem)
    rq = z.d // z.n_dp
    qc = z.d // z.n_dp
    meet(
        [p.hdev(i) for i in range(1, z.H)]
        + [p.xdev(i) for i in range(1, z.X)]
        + [p.y(), p.core()]
    )
    c_out = []
    for k in range(z.X):
        x = p.xi(k)
        c_out.append(
            (
                net.remote(do.at[:, :, part(x * 2 + 1 - p.c, qc)], oc.at[k], p.core()),
                net.remote(dw.at[:, :, part(x * 2 + 1 - p.c, rq)], wc.at[k], p.core()),
            )
        )
    for k in list(range(1, z.X)) + [0]:
        for cp in c_out[k]:
            cp.start()
    x_out = []
    for k in list(range(1, z.X)) + [0]:
        for cp in c_out[k]:
            cp.wait_recv()
        x = p.xi(k)
        for r in range(z.G):
            os_[k, r] = add_refs(do[r, :, part(x * 2 + p.c, qc)], oc[k, r]).astype(BF16)
        for g in range(z.NG):
            ws[k, g] = add_refs(dw[g, :, part(x * 2 + p.c, rq)], wc[k, g]).astype(BF16)
        if k:
            pair = (
                net.remote(os_.at[k], ox.at[k - 1], p.xdev(k)),
                net.remote(ws.at[k], wx.at[k - 1], p.xdev(k)),
            )
            for cp in pair:
                cp.start()
            x_out.append(pair)
    for pair in x_out:
        for cp in pair:
            cp.wait_recv()
    for r in range(z.G):
        os_[0, r] = add_refs(os_[0, r], *[ox[i, r] for i in range(z.X - 1)]).astype(BF16)
    y_out = []
    for k in range(z.G // 2):
        y_out.append(net.remote(os_.at[0, k * 2 + 1 - p.lo], oy.at[k], p.y()))
        y_out[-1].start()
    for g in range(z.NG):
        ws[0, g] = add_refs(ws[0, g], *[wx[i, g] for i in range(z.X - 1)]).astype(BF16)
    g_out = []
    for i in range(1, z.NG):
        g_out.append(net.remote(ws.at[0, p.gi(i)], wg.at[i - 1], p.gdev(i)))
        g_out[-1].start()
    for cp in y_out:
        cp.wait_recv()
    for k in range(z.G // 2):
        oy_sum[k] = add_refs(os_[0, k * 2 + p.lo], oy[k]).astype(BF16)
    z_out = []
    half = z.G // 2
    for i in range(1, z.H):
        hi = p.hii(i)
        z_out.append(
            net.remote(oy_sum.at[hi % half, part(hi // half, z.cw)], oz.at[i - 1], p.hdev(i))
        )
        z_out[-1].start()
    for cp in g_out:
        cp.wait_recv()
    quarter = part(p.dp, rq)
    for m in range(3):
        ow[m, quarter] = add_refs(ws[0, p.g, m], *[wg[i, m] for i in range(z.NG - 1)]).astype(BF16)
    for cp in z_out:
        cp.wait_recv()
    cols = part(p.dp, qc)
    oo[:, cols] = add_refs(
        oy_sum[p.hi % half, part(p.hi // half, z.cw)], *[oz[i] for i in range(z.H - 1)]
    ).astype(BF16)
    along = []
    for i in range(1, z.X):
        for block in (ow.at[:, quarter], oo.at[:, cols]):
            along.append(net.remote(block, block, p.xdev(i)))
            along[-1].start()
    for cp in along:
        cp.wait_recv()
    across = []
    for x in range(z.X):
        for block in (ow.at[:, part(x * 2 + p.c, rq)], oo.at[:, part(x * 2 + p.c, qc)]):
            across.append(net.remote(block, block, p.core()))
            across[-1].start()
    for cp in across:
        cp.wait_recv()
    net.wait_sends()


def lane_of(rows):
    return lax.broadcasted_iota(jnp.int32, (rows, 128), 1)


def rope_tables():
    frequency = np.float32(10000.0) ** (-np.arange(HD // 2, dtype=np.float32) * 2.0 / HD)
    angles = np.arange(WIN, dtype=np.float32)[:, None] * frequency.astype(np.float32)[None, :]
    angles = np.concatenate([angles] * 4, axis=1)
    return np.cos(angles), np.sin(angles)


def turn(v, cosines, sines):
    swapped = jnp.where(
        lane_of(v.shape[0]) % HD < HD // 2, -pltpu.roll(v, 96, 1), pltpu.roll(v, 32, 1)
    )
    return v * cosines + swapped * sines


def spare_lanes(first, v, lane):
    high = v.astype(BF16)
    rest = v - high.astype(F32)
    middle = rest.astype(BF16)
    low = (rest - middle.astype(F32)).astype(BF16)
    s = lane % HD
    tail = jnp.where(s == 2, -middle.astype(F32), jnp.where(s == 3, -low.astype(F32), 0.0))
    return jnp.where(s == 0, first, jnp.where(s == 1, -high.astype(F32), tail))


def forward_kernel(n1, w3, cos, sin, bias, q, k, v, o, mixed, qa, *, bq):
    width = q.shape[1]
    chunk = 512

    def project(i, _):
        rows = part(i, chunk)
        a = n1[rows]
        for m, ref in enumerate((q, k, v)):
            y = dot(a, w3[m])
            for j in range(width // 128):
                t = y[:, j * 128 : j * 128 + 128]
                if m < 2:
                    t = turn(t, cos[rows], sin[rows])
                ref[rows, j * 128 : j * 128 + 128] = t.astype(BF16)
        return 0

    lax.fori_loop(0, WIN // chunk, project, 0)
    lane_k, lane_q = lane_of(WIN), lane_of(bq)

    def block(i, _):
        j, b = i // (WIN // bq), i % (WIN // bq)
        col, rows = part(j, 128), part(b, bq)
        k2, v2, kb, q2 = k[:, col], v[:, col], bias[...], q[rows, col]
        mixes = []
        for e in range(2):
            own_k = (lane_k < HD) if e == 0 else (lane_k >= HD)
            own_q = (lane_q < HD) if e == 0 else (lane_q >= HD)
            k_e = jnp.where(own_k, k2, kb)
            v_e = jnp.where(own_k, v2, jnp.ones_like(v2))
            q_e = jnp.where(own_q, q2, jnp.where(lane_q % HD == 0, 1.0, 0.0).astype(BF16))
            s = dot(q_e, k_e, NT)
            top = jnp.max(s, axis=1, keepdims=True)
            p = jnp.exp2((s - top) * C2).astype(BF16)
            sums = dot(p, v_e)
            mixes.append(sums / pltpu.roll(sums, HD, 1))
            norm = jnp.where(own_q, 0.0, top + jnp.log2(jnp.where(own_q, 1.0, sums)) * (1.0 / C2))
            full = jnp.where(own_q, q2.astype(F32), spare_lanes(1.0, norm, lane_q))
            qa[2 * j + e, rows] = full.astype(BF16)
        mix = jnp.where(lane_q < HD, mixes[0], mixes[1])
        o[rows, col] = mix
        mixed[rows, col] = mix.astype(BF16)
        return 0

    lax.fori_loop(0, (width // 128) * (WIN // bq), block, 0)


def attend_forward(n1, w3, cos, sin, bias):
    hw = w3.shape[2]
    return pl.pallas_call(
        functools.partial(forward_kernel, bq=256),
        out_shape=(
            shape((WIN, hw)),
            shape((WIN, hw)),
            shape((WIN, hw)),
            shape((WIN, hw), F32),
            shape((WIN, hw)),
            shape((hw // HD, WIN, 128)),
        ),
        in_specs=[VMEM] * 5,
        out_specs=[VMEM] * 6,
        compiler_params=pltpu.CompilerParams(vmem_limit_bytes=60 * MIB),
        name="attend_forward",
    )(n1, w3, cos, sin, bias)


def backward_kernel(qa, q, k, v, do, o, bias, cos, sin, dq, dk, dv, do_e, dk_sum, dv_sum, *, bq):
    width = q.shape[1]
    lane_q, lane_k = lane_of(bq), lane_of(WIN)
    blocks = WIN // bq

    def block(i, _):
        j, b = i // blocks, i % blocks
        col, rows = part(j, 128), part(b, bq)
        q2, do2, k2, v2 = q[rows, col], do[rows, col], k[:, col], v[:, col]
        prod = do2.astype(F32) * o[rows, col]
        s64 = lane_k % HD
        ones3 = jnp.where((s64 >= 1) & (s64 <= 3), 1.0, 0.0).astype(BF16)
        kb = bias[...] + ones3
        dks, dvs, dqs = [], [], []
        for e in range(2):
            own_q = (lane_q < HD) if e == 0 else (lane_q >= HD)
            own_k = (lane_k < HD) if e == 0 else (lane_k >= HD)
            delta = jnp.sum(jnp.where(own_q, prod, 0.0), axis=1, keepdims=True)
            spare = spare_lanes(0.0, jnp.broadcast_to(delta, prod.shape), lane_q)
            do_e[...] = jnp.where(own_q, do2.astype(F32), spare).astype(BF16)
            k_e = jnp.where(own_k, k2, kb)
            v_e = jnp.where(own_k, v2, ones3)
            p = jnp.exp2(dot(k_e, qa[2 * j + e, rows], NT) * C2)
            ds = (p * dot(v_e, do_e[...], NT)).astype(BF16)
            dvs.append(dot(p.astype(BF16), do2))
            dks.append(dot(ds, q2))
            dqs.append(dot(ds, k2, TN))
        dv_new = jnp.where(lane_k < HD, dvs[0], dvs[1])
        dk_new = jnp.where(lane_k < HD, dks[0], dks[1])

        @pl.when(b == 0)
        def _():
            dv_sum[...] = dv_new
            dk_sum[...] = dk_new

        @pl.when(b > 0)
        def _():
            dv_sum[...] += dv_new
            dk_sum[...] += dk_new

        dq_new = jnp.where(lane_q < HD, dqs[0], dqs[1]) * SCALE
        dq[rows, col] = turn(dq_new, cos[rows], -sin[rows]).astype(BF16)

        @pl.when(b == blocks - 1)
        def _():
            dv[:, col] = dv_sum[...].astype(BF16)
            dk[:, col] = turn(dk_sum[...] * SCALE, cos[...], -sin[...]).astype(BF16)

        return 0

    lax.fori_loop(0, (width // 128) * blocks, block, 0)


def attend_backward(qa, q, k, v, do, o, bias, cos, sin):
    hw = q.shape[1]
    bq = 512
    return pl.pallas_call(
        functools.partial(backward_kernel, bq=bq),
        out_shape=(shape((WIN, hw)),) * 3,
        in_specs=[VMEM] * 9,
        out_specs=[VMEM] * 3,
        scratch_shapes=[
            pltpu.VMEM((bq, 128), BF16),
            pltpu.VMEM((WIN, 128), F32),
            pltpu.VMEM((WIN, 128), F32),
        ],
        compiler_params=pltpu.CompilerParams(vmem_limit_bytes=60 * MIB),
        name="attend_backward",
    )(qa, q, k, v, do, o, bias, cos, sin)


def norm_stats(v):
    centre = v - jnp.mean(v, axis=-1, keepdims=True)
    inverse = lax.rsqrt(jnp.mean(centre * centre, axis=-1, keepdims=True) + EPSILON)
    return centre * inverse, inverse


def norm_backward(grad_in, scaled, inverse, gain):
    weighted = grad_in * gain
    first_mean = jnp.mean(weighted, axis=-1, keepdims=True)
    second_mean = jnp.mean(weighted * scaled, axis=-1, keepdims=True)
    return inverse * (weighted - first_mean - scaled * second_mean)


def per_device(
    n_dp, n_t, tokens, lengths, ln1_gain, ln1_bias, w_query, w_key, w_value, w_out,
    ln2_gain, ln2_bias, w_gate, w_up, w_down, cotangent,
):
    rows, d = tokens.shape
    cw, cfull = w_query.shape[1], w_gate.shape[1]
    z = Sizes(n_dp, n_t, rows, d, cw, cfull)
    G, NG, H, X, hw, cf = z.G, z.NG, z.H, z.X, z.hw, z.cf
    rq, rx, dx = d // n_dp, d // X, cf // X
    slot = lax.axis_index("tensor") // G
    length = lax.dynamic_index_in_dim(lengths, slot, keepdims=False)
    lane = lax.broadcasted_iota(jnp.int32, (WIN, 128), 1) % HD
    place = lax.broadcasted_iota(jnp.int32, (WIN, 128), 0)
    bias = jnp.where((lane == 0) & (place >= length), -1e30, 0.0).astype(BF16)
    cos, sin = (jnp.asarray(t, F32) for t in rope_tables())

    own_tokens = tokens.astype(F32)
    scaled_one, inverse_one = norm_stats(own_tokens)
    normed_one = (scaled_one * ln1_gain + ln1_bias).astype(BF16)
    w_three = jnp.stack([w_query, w_key, w_value])
    n1, w3 = comm_call(
        gather_rows_kernel, z, "gather_rows", 1,
        (shape((WIN, d)), shape((NG, 3, d, cw))), [HBM] * 2, [HBM] * 2,
    )(normed_one, w_three)
    wo, wg, wu, wd = comm_call(
        gather_weights_kernel, z, "gather_weights", 2,
        (shape((d, d)), shape((d, H * cf)), shape((d, H * cf)), shape((H * cf, d))),
        [HBM] * 4, [HBM] * 4, n=96,
    )(w_out, w_gate, w_up, w_down)
    w3 = jnp.transpose(w3, (1, 2, 0, 3)).reshape(3, d, hw)
    q, k, v, o, mixed, qa = attend_forward(n1, w3, cos, sin, bias)
    mixed_own = comm_call(
        mixed_kernel, z, "mixed_rows", 3, shape((rows, d)), [HBM], HBM
    )(mixed)
    middle = own_tokens + dot(mixed_own, wo)
    scaled_two, inverse_two = norm_stats(middle)
    normed_two = (scaled_two * ln2_gain + ln2_bias).astype(BF16)

    four = functools.partial(comm_call, gather_four_kernel, z)
    seed = four("gather_seed", 4, shape((4, rows, d)), [HBM], HBM)(cotangent)
    n2 = four("gather_normed", 5, shape((4, rows, d)), [HBM], HBM)(normed_two)
    seed, n2 = seed.reshape(4 * rows, d), n2.reshape(4 * rows, d)
    gate, up = dot(n2, wg), dot(n2, wu)
    sig = jax.nn.sigmoid(gate)
    silu = gate * sig
    hidden = (silu * up).astype(BF16)
    part_out = dot(hidden, wd).astype(BF16)
    grad_hidden = dot(seed, wd, NT)
    grad_gate = (grad_hidden * up * sig * (1.0 + gate * (1.0 - sig))).astype(BF16)
    grad_up = (grad_hidden * silu).astype(BF16)
    part_two = (dot(grad_gate, wg, NT) + dot(grad_up, wu, NT)).astype(BF16)
    p_down = dot(hidden, seed, TN).astype(BF16).reshape(H, cf, d)
    p_gate = dot(n2, grad_gate, TN).astype(BF16)
    p_up = dot(n2, grad_up, TN).astype(BF16)
    ffn, grad_two = comm_call(
        scatter_four_kernel, z, "scatter_four", 6,
        (shape((rows, d), F32), shape((rows, d), F32)), [VMEM] * 2, [VMEM] * 2,
        [
            pltpu.VMEM((2, 2, rows, d), BF16),
            pltpu.VMEM((2, rows, d), BF16),
            pltpu.VMEM((2, rows, d), BF16),
        ],
        vmem=60 * MIB,
    )(part_out.reshape(4, rows, d), part_two.reshape(4, rows, d))
    output = (middle + ffn).astype(BF16)
    gain_two = jnp.sum(grad_two * scaled_two, axis=0)
    bias_two = jnp.sum(grad_two, axis=0)
    grad_middle = cotangent.astype(F32) + norm_backward(grad_two, scaled_two, inverse_two, ln2_gain)
    grad_low = grad_middle.astype(BF16)
    p_wo = dot(mixed_own, grad_low, TN).astype(BF16).reshape(G, hw, d)
    grad_mixed = dot(grad_low, wo, NT).astype(BF16)
    do = comm_call(unmix_kernel, z, "unmix_rows", 7, shape((WIN, hw)), [HBM], HBM)(grad_mixed)
    g_gate, g_up, g_down = comm_call(
        reduce_ffn_kernel, z, "reduce_ffn", 8,
        (shape((d, 2 * cf)), shape((d, 2 * cf)), shape((2 * cf, d))), [VMEM] * 3, [VMEM] * 3,
        [
            pltpu.VMEM((X - 1, rx, H * cf), BF16),
            pltpu.VMEM((X - 1, rx, H * cf), BF16),
            pltpu.VMEM((X - 1, H, dx, d), BF16),
            pltpu.VMEM((rx, H * cf), BF16),
            pltpu.VMEM((rx, H * cf), BF16),
            pltpu.VMEM((H, dx, d), BF16),
            pltpu.VMEM((H - 1, rx, cf), BF16),
            pltpu.VMEM((H - 1, rx, cf), BF16),
            pltpu.VMEM((H - 1, dx, d), BF16),
        ],
        vmem=60 * MIB,
    )(p_gate, p_up, p_down)
    dq, dk, dv = attend_backward(qa, q, k, v, do, o, bias, cos, sin)
    part_one = (dot(dq, w3[0], NT) + dot(dk, w3[1], NT) + dot(dv, w3[2], NT)).astype(BF16)
    got = comm_call(
        scatter_rows_kernel, z, "scatter_rows", 9, shape((G, rows, d)), [HBM], HBM
    )(part_one.reshape(G, rows, d))
    p_w3 = jnp.stack([dot(n1, t, TN).astype(BF16) for t in (dq, dk, dv)])
    p_w3 = jnp.transpose(p_w3.reshape(3, d, NG, cw), (2, 0, 1, 3))
    g_w3, g_wo = comm_call(
        reduce_attn_kernel, z, "reduce_attn", 10,
        (shape((3, d, cw)), shape((cw, d))), [VMEM] * 2, [VMEM] * 2,
        [
            pltpu.VMEM((X, NG, 3, rq, cw), BF16),
            pltpu.VMEM((X - 1, NG, 3, rq, cw), BF16),
            pltpu.VMEM((X, NG, 3, rq, cw), BF16),
            pltpu.VMEM((NG - 1, 3, rq, cw), BF16),
            pltpu.VMEM((X, G, hw, rq), BF16),
            pltpu.VMEM((X - 1, G, hw, rq), BF16),
            pltpu.VMEM((X, G, hw, rq), BF16),
            pltpu.VMEM((G // 2, hw, rq), BF16),
            pltpu.VMEM((G // 2, hw, rq), BF16),
            pltpu.VMEM((H - 1, cw, rq), BF16),
        ],
        vmem=60 * MIB,
    )(p_w3, p_wo)
    grad_one = jnp.sum(got.astype(F32), axis=0)
    gain_one = jnp.sum(grad_one * scaled_one, axis=0)
    bias_one = jnp.sum(grad_one, axis=0)
    back_one = norm_backward(grad_one, scaled_one, inverse_one, ln1_gain)
    grad_tokens = (grad_middle + back_one).astype(BF16)
    norms = lax.psum(jnp.stack([gain_one, bias_one, gain_two, bias_two]), ("dp", "tensor"))
    return (
        output, grad_tokens, norms[0], norms[1],
        g_w3[0].astype(F32), g_w3[1].astype(F32), g_w3[2].astype(F32), g_wo.astype(F32),
        norms[2], norms[3], g_gate.astype(F32), g_up.astype(F32), g_down.astype(F32),
    )


def solution(mesh):
    rows, cols, each = P(("dp", "tensor"), None), P(None, "tensor"), P("tensor", None)
    return jax.shard_map(
        functools.partial(per_device, mesh.shape["dp"], mesh.shape["tensor"]),
        mesh=mesh,
        in_specs=(
            rows, P("dp"), P(), P(), cols, cols, cols, each, P(), P(), cols, cols, each, rows,
        ),
        out_specs=(
            rows, rows, P(), P(), cols, cols, cols, each, P(), P(), cols, cols, each,
        ),
        check_vma=False,
    )
```

time: 1990 us -> 847 us (0.43)
  waiting for transfers between devices: 1020 us -> 0 us
  Pallas kernels: 0 us -> 654 us
  matrix products: 511 us -> 97.5 us
  local copies, waits for them, and re-layouts: 210 us -> 13.6 us
  other arithmetic: 162 us -> 36.8 us
    pallas_call x0 -> x12, Pallas kernels: none -> 654 us  [the longest x1 119 us: per_device(): comm_call(reduce_ffn_kernel, z, 'reduce_ffn', 8, (shape((d, 2 * cf)), sha...]
    psum x3 -> x0, waiting for transfers between devices: 527 us -> none  [the longest x1 268 us: per_device(): lax.psum(jnp.dot(mixed_low, w_out, preferred_element_type=jnp.float32).as...]
    dot_general x77 -> x18, matrix products: 511 us -> 97.5 us  [dot(): return lax.dot_general(a, b, dims, preferred_element_type=F32)]
    reduce_scatter x2 -> x0, waiting for transfers between devices: 287 us -> none  [the longest x1 148 us: per_device(): lax.psum_scatter((summed + lax.dot_general(grad_values, w_value, LAST_DIM...]
    all_gather x2 -> x0, waiting for transfers between devices: 202 us -> none  [the longest x1 121 us: per_device(): lax.all_gather(tokens, 'tensor', axis=0, tiled=True).astype(jnp.float32)]
    dynamic_update_slice x10 -> x0, local copies, waits for them, and re-layouts: 89.2 us -> none  [attend_backward(): lax.map(one_slot, (queries.reshape(block_shape), grad_mixed.reshape(block...]
    convert_element_type x15 -> x9, other arithmetic: 61 us -> 17.6 us  [the longest x1 3.29 us: per_device(): grad_tokens = (grad_middle + back_one).astype(BF16)]
    while x66 -> x0, local copies, waits for them, and re-layouts: 39.9 us -> none
  transfers between devices with their start and end apart: 7 -> 0, of which waited for: 7 -> 0; matrix products, arithmetic and copies ran while one was open for 8% -> 0% of each run, Pallas kernels for 0% -> 0%
where the time goes in v1:
time: 847 us; the launch traced here: 843 us
  Pallas kernels  654 us (77%)
  matrix products  97.5 us (12%)
  blocking collectives  40 us (5%)
  other arithmetic  36.8 us (4%)
  local copies, waits for them, and re-layouts  13.6 us (2%)
    pallas_call x1, Pallas kernels, per_device(): comm_call(reduce_ffn_kernel, z, 'reduce_ffn', 8, (shape((d, 2 * cf)), sha...  119 us
    pallas_call x1, Pallas kernels, per_device(): comm_call(gather_weights_kernel, z, 'gather_weights', 2, (shape((d, d)),...  110 us
    dot_general x18, matrix products, dot(): return lax.dot_general(a, b, dims, preferred_element_type=F32)  97.5 us
    pallas_call x1, Pallas kernels, per_device(): comm_call(scatter_four_kernel, z, 'scatter_four', 6, (shape((rows, d), F3...  57.7 us
    pallas_call x1, Pallas kernels, per_device(): comm_call(gather_rows_kernel, z, 'gather_rows', 1, (shape((WIN, d)), shap...  57 us
    pallas_call x1, Pallas kernels, attend_backward(): pl.pallas_call(functools.partial(backward_kernel, bq=bq), out_shape=(shap...  56.7 us
    pallas_call x1, Pallas kernels, per_device(): comm_call(reduce_attn_kernel, z, 'reduce_attn', 10, (shape((3, d, cw)), s...  54.2 us
    pallas_call x1, Pallas kernels, per_device(): comm_call(scatter_rows_kernel, z, 'scatter_rows', 9, shape((G, rows, d)),...  51 us

profile of v1, /device:TPU:0, one launch (start us, length us, event | category | flops | bytes accessed | tf_op | source)
XLA Modules:
  0.0 843.1 jit_solution(5736675678651975015)
XLA Ops:
  9.5 57.0 %gather_rows.1 = (bf16[2048,1024]{1,0:T(8,128)(2,1)}, bf16[2,3,1024,128]{3,2,1,0:T(8,128)(2,1)}) custom-call(bf16[512,1024]{1,0:T(8,128)(2,1)} %fusion.12.n1, bf16[3,1024,128]{2,1,0:T(8,128)(2,1)} %pad_maximum_fusion.w3), custom_call_target="tpu_custom_call" | custom-call | tf_op jit(solution)/shard_map/gather_rows/pallas_call | solution.py:731
  72.5 35.7 %gather_seed.1 = bf16[4,512,1024]{2,1,0:T(8,128)(2,1)} custom-call(bf16[512,1024]{1,0:T(8,128)(2,1)} %own.1), custom_call_target="tpu_custom_call" | custom-call | tf_op jit(solution)/shard_map/gather_seed/pallas_call | solution.py:750
  108.3 39.6 %attend_forward.1 = (bf16[2048,256]{1,0:T(8,128)(2,1)}, bf16[2048,256]{1,0:T(8,128)(2,1)}, bf16[2048,256]{1,0:T(8,128)(2,1)}, f32[2048,256]{1,0:T(8,128)}, bf16[...) custom-call(bf16[2048,1024]{1,0:T(8,128)(2,1)} %get-tuple-element.35.n1, bf16[3,1024,256]{2,1,0:T(8,128)(2,1)} %copy_bitcast_fusion.w3, ...), custom_call_target="tpu_custom_call" | custom-call | tf_op jit(solution)/shard_map/attend_forward/pallas_call | solution.py:610
  147.9 16.5 %mixed_rows.1 = bf16[512,1024]{1,0:T(8,128)(2,1)} custom-call(bf16[2048,256]{1,0:T(8,128)(2,1)} %get-tuple-element.37.mixed), custom_call_target="tpu_custom_call" | custom-call | tf_op jit(solution)/shard_map/mixed_rows/pallas_call | solution.py:742
  164.4 110.4 %gather_weights.1 = (bf16[1024,1024]{1,0:T(8,128)(2,1)}, bf16[1024,1024]{1,0:T(8,128)(2,1)}, bf16[1024,1024]{1,0:T(8,128)(2,1)}, bf16[1024,1024]{1,0:T(8,128)(2,1)}) custom-call(bf16[128,1024]{1,0:T(8,128)(2,1)} %wo.1, bf16[1024,512]{1,0:T(8,128)(2,1)} %wg.1, bf16[1024,512]{1,0:T(8,128)(2,1)} %wu.1, bf16[512,1024]{1,0:T(8,128)(2,1)} %wd.1), custom_call_target="tpu_custom_call" | custom-call | tf_op jit(solution)/shard_map/gather_weights/pallas_call | solution.py:735
  280.2 35.3 %gather_normed.1 = bf16[4,512,1024]{2,1,0:T(8,128)(2,1)} custom-call(bf16[512,1024]{1,0:T(8,128)(2,1)} %add_convert_fusion.3.own), custom_call_target="tpu_custom_call" | custom-call | tf_op jit(solution)/shard_map/gather_normed/pallas_call | solution.py:751
  315.5 10.8 %fusion.27 = f32[2048,1024]{1,0:T(8,128)} fusion(bf16[2048,1024]{1,0:T(8,128)(2,1)} %bitcast.91, bf16[1024,1024]{1,0:T(8,128)(2,1)} %get-tuple-element.40), kind=kOutput, calls=%fused_computation.77 | convolution fusion | flops 4294967296 | bytes 14680064 | tf_op jit(solution)/shard_map/dot_general | solution.py:29
  326.3 7.1 fusion.26
  333.4 14.6 %fusion.3 = (bf16[2048,1024]{1,0:T(8,128)(2,1)}, bf16[2048,1024]{1,0:T(8,128)(2,1)}, bf16[2048,1024]{1,0:T(8,128)(2,1)}) fusion(f32[2048,1024]{1,0:T(8,128)} %fusion.26, f32[2048,1024]{1,0:T(8,128)} %fusion.27, bf16[1024,1024]{1,0:T(8,128)(2,1)S(1)} %copy-done.33, bf16[2048,1024]{1,0:T(8,128)(2,1)S(1)} %bitcast.89), kind=kOutput, calls=%fused_computation.7 | convolution fusion | flops 4326424576 | bytes 35651584 | tf_op jit(solution)/shard_map/dot_general | solution.py:29
  348.0 8.1 convolution_convert_fusion.1
  356.1 5.7 convolution_convert_fusion.2.du
  361.8 5.7 convolution_convert_fusion.3.dg
  367.6 118.5 %reduce_ffn.1 = (bf16[1024,512]{1,0:T(8,128)(2,1)}, bf16[1024,512]{1,0:T(8,128)(2,1)}, bf16[512,1024]{1,0:T(8,128)(2,1)}) custom-call(bf16[1024,1024]{1,0:T(8,128)(2,1)} %convolution_convert_fusion.3.dg, bf16[1024,1024]{1,0:T(8,128)(2,1)} %convolution_convert_fusion.2.du, bf16[4,256,1024]{2,1,0:T(8,128)(2,1)} %bitcast.97), custom_call_target="tpu_custom_call" | custom-call | tf_op jit(solution)/shard_map/reduce_ffn/pallas_call | solution.py:783
  493.1 7.3 fusion.28
  500.4 8.7 %add_convert_fusion.1 = bf16[2048,1024]{1,0:T(8,128)(2,1)} fusion(f32[2048,1024]{1,0:T(8,128)} %fusion.28, bf16[2048,1024]{1,0:T(8,128)(2,1)S(1)} %copy-done.40, bf16[1024,1024]{1,0:T(8,128)(2,1)S(1)} %copy-done.35), kind=kOutput, calls=%fused_computation.9 | convolution fusion | flops 4299161600 | bytes 18874368 | tf_op jit(solution)/shard_map/dot_general | solution.py:29
  509.1 6.0 convolution_convert_fusion
  515.1 57.7 %scatter_four.1 = (f32[512,1024]{1,0:T(8,128)}, f32[512,1024]{1,0:T(8,128)}) custom-call(bf16[4,512,1024]{2,1,0:T(8,128)(2,1)} %bitcast.96, bf16[4,512,1024]{2,1,0:T(8,128)(2,1)} %bitcast.95), custom_call_target="tpu_custom_call" | custom-call | tf_op jit(solution)/shard_map/scatter_four/pallas_call | solution.py:765
  581.2 20.9 %unmix_rows.1.do = bf16[2048,256]{1,0:T(8,128)(2,1)} custom-call(bf16[512,1024]{1,0:T(8,128)(2,1)} %convolution_convert_fusion.5.own), custom_call_target="tpu_custom_call" | custom-call | tf_op jit(solution)/shard_map/unmix_rows/pallas_call | solution.py:782
  602.1 56.7 %attend_backward.1 = (bf16[2048,256]{1,0:T(8,128)(2,1)}, bf16[2048,256]{1,0:T(8,128)(2,1)}, bf16[2048,256]{1,0:T(8,128)(2,1)}) custom-call(bf16[4,2048,128]{2,1,0:T(8,128)(2,1)} %get-tuple-element.44.qa, bf16[2048,256]{1,0:T(8,128)(2,1)} %get-tuple-element.45.q, bf16[2048,256]{1,0:T(8,128)(2,1)} %get-tuple-element.46.k, ...), custom_call_target="tpu_custom_call" | custom-call | tf_op jit(solution)/shard_map/attend_backward/pallas_call | solution.py:683
  663.7 4.4 convolution_convert_fusion.7
  678.1 54.2 %reduce_attn.1 = (bf16[3,1024,128]{2,1,0:T(8,128)(2,1)}, bf16[128,1024]{1,0:T(8,128)(2,1)}) custom-call(bf16[2,3,1024,128]{3,2,1,0:T(8,128)(2,1)} %maximum_bitcast_fusion.dw, bf16[4,256,1024]{2,1,0:T(8,128)(2,1)} %bitcast.98), custom_call_target="tpu_custom_call" | custom-call | tf_op jit(solution)/shard_map/reduce_attn/pallas_call | solution.py:806
  742.5 51.0 %scatter_rows.1 = bf16[4,512,1024]{2,1,0:T(8,128)(2,1)} custom-call(bf16[4,512,1024]{2,1,0:T(8,128)(2,1)} %bitcast.87), custom_call_target="tpu_custom_call" | custom-call | tf_op jit(solution)/shard_map/scatter_rows/pallas_call | solution.py:801
  793.5 4.3 convert_reduce_fusion
  798.8 40.0 %psum.7 = f32[4,1024]{1,0:T(4,128)S(1)} all-reduce(f32[4,1024]{1,0:T(4,128)S(1)} %pad_maximum_fusion.1), channel_id=1, replica_groups=mesh['dp'=4,'tensor'=8] {'dp','tensor'}, use_global_device_ids=true, to_apply=%region_13.14 | all-reduce | flops 4096 | bytes 32768 | tf_op jit(solution)/shard_map/psum | solution.py:828
  (133 shorter events, 65.2 us)
Async XLA Ops:
  0.6 6.4 copy-start.20
  0.7 6.4 copy-start.21
  0.7 6.4 copy-start.22
  2.7 5.4 copy-start
  2.7 5.3 copy-start.26
  2.7 5.3 copy-start.30
  315.5 10.8 %copy-start.6 = (bf16[4,512,1024]{2,1,0:T(8,128)(2,1)S(1)}, bf16[4,512,1024]{2,1,0:T(8,128)(2,1)}, u32[]{:S(2)}) copy-start(bf16[4,512,1024]{2,1,0:T(8,128)(2,1)} %gather_normed.1) | copy-start | bytes 12582916
  315.5 10.8 %copy-start.36 = (bf16[1024,1024]{1,0:T(8,128)(2,1)S(1)}, bf16[1024,1024]{1,0:T(8,128)(2,1)}, u32[]{:S(2)}) copy-start(bf16[1024,1024]{1,0:T(8,128)(2,1)} %get-tuple-element.39) | copy-start | bytes 6291460
  326.3 7.1 copy-start.5
  326.3 7.1 copy-start.33
  348.0 8.1 copy-start.39
  356.1 5.7 copy-start.41
  486.1 6.2 copy-start.42
  493.1 7.3 copy-start.35
  493.1 7.3 copy-start.40
  500.4 8.7 %copy-start.34 = (bf16[1024,1024]{1,0:T(8,128)(2,1)S(1)}, bf16[1024,1024]{1,0:T(8,128)(2,1)}, u32[]{:S(2)}) copy-start(bf16[1024,1024]{1,0:T(8,128)(2,1)} %get-tuple-element.41) | copy-start | bytes 6291460
  500.4 8.7 %copy-start.38 = (bf16[2048,1024]{1,0:T(8,128)(2,1)S(1)}, bf16[2048,1024]{1,0:T(8,128)(2,1)}, u32[]{:S(2)}) copy-start(bf16[2048,1024]{1,0:T(8,128)(2,1)} %get-tuple-element.68) | copy-start | bytes 12582916
  658.9 4.9 copy-start.13
  663.7 4.4 copy-start.7
  663.7 4.4 copy-start.15
  670.5 5.0 copy-start.3
  793.5 4.3 copy-start.24
  793.5 4.3 copy-start.27
  793.5 4.3 copy-start.29
  (19 other events, 44.7 us)

commit v2 on v0

v2 whole, which is shorter than its diff:
```python
import functools

import jax
import jax.numpy as jnp
import numpy as np
from jax import lax
from jax.experimental import pallas as pl
from jax.experimental.pallas import tpu as pltpu
from jax.sharding import PartitionSpec as P

HD = 64
WIN = 2048
EPSILON = 1e-05
SCALE = HD ** (-0.5)
LOG2E = 1.4426950408889634
C2 = SCALE * LOG2E
NT = (((1,), (1,)), ((), ()))
NN = (((1,), (0,)), ((), ()))
TN = (((0,), (0,)), ((), ()))
MESH = pl.DeviceIdType.MESH
F32 = jnp.float32
BF16 = jnp.bfloat16
MIB = 1024 * 1024
HBM = pl.BlockSpec(memory_space=pl.ANY)
VMEM = pl.BlockSpec(memory_space=pltpu.VMEM)


def dot(a, b, dims=NN):
    return lax.dot_general(a, b, dims, preferred_element_type=F32)


def shape(dims, kind=BF16):
    return jax.ShapeDtypeStruct(dims, kind)


class Sizes:
    def __init__(self, n_dp, n_t, rows, d, cw, cfull):
        self.n_dp, self.n_t, self.rows, self.d = n_dp, n_t, rows, d
        self.X, self.H = n_dp // 2, n_t // 2
        self.G = WIN // rows
        self.NG = n_t // self.G
        self.cw, self.hw = cw, self.NG * cw
        self.cf = cfull // 2


class Place:
    def __init__(self, z):
        self.z = z
        dp, t = lax.axis_index("dp"), lax.axis_index("tensor")
        self.dp, self.t = dp, t
        self.x, self.c = dp // 2, dp % 2
        self.hi, self.lo = t // 2, t % 2
        self.g, self.r = t // z.G, t % z.G
        self.h2, self.hl = self.hi // 2, self.hi % 2

    def pair(self):
        return (self.dp, (self.h2 * 2 + 1 - self.hl) * 2 + self.lo)

    def h2dev(self, i):
        return (self.dp, (((self.h2 + i) % (self.z.H // 2)) * 2 + self.hl) * 2 + self.lo)

    def core(self):
        return (self.x * 2 + 1 - self.c, self.t)

    def y(self):
        return (self.dp, self.hi * 2 + 1 - self.lo)

    def xi(self, i):
        return (self.x + i) % self.z.X

    def xdev(self, i):
        return (self.xi(i) * 2 + self.c, self.t)

    def hii(self, i):
        return (self.hi + i) % self.z.H

    def hdev(self, i):
        return (self.dp, self.hii(i) * 2 + self.lo)

    def ri(self, i):
        return (self.r + i) % self.z.G

    def rdev(self, i):
        return (self.dp, self.g * self.z.G + self.ri(i))

    def gi(self, i):
        return (self.g + i) % self.z.NG

    def gdev(self, i):
        return (self.dp, self.gi(i) * self.z.G + self.r)


class Net:
    def __init__(self, send, recv, local=None):
        self.send, self.recv, self.local_sem = send, recv, local
        self.count, self.local_count = 0, 0
        self.all = []

    def remote(self, src, dst, device):
        k = self.count
        self.count += 1
        cp = pltpu.make_async_remote_copy(
            src_ref=src, dst_ref=dst, send_sem=self.send.at[k], recv_sem=self.recv.at[k],
            device_id=device, device_id_type=MESH,
        )
        self.all.append(cp)
        return cp

    def local(self, src, dst):
        k = self.local_count
        self.local_count += 1
        return pltpu.make_async_copy(src, dst, self.local_sem.at[k])

    def wait_sends(self):
        for cp in self.all:
            cp.wait_send()


def meet(devices):
    barrier = pltpu.get_barrier_semaphore()
    for device in devices:
        pl.semaphore_signal(barrier, inc=1, device_id=device, device_id_type=MESH)
    pl.semaphore_wait(barrier, len(devices))


def part(i, n):
    return pl.ds(pl.multiple_of(i * n, n), n)


def comm_call(body, z, name, cid, out_shape, in_specs, out_specs, scratch=(), n=64, vmem=None):
    return pl.pallas_call(
        functools.partial(body, z),
        out_shape=out_shape,
        in_specs=in_specs,
        out_specs=out_specs,
        scratch_shapes=[
            pltpu.SemaphoreType.DMA((n,)),
            pltpu.SemaphoreType.DMA((n,)),
            pltpu.SemaphoreType.DMA((64,)),
            *scratch,
        ],
        compiler_params=pltpu.CompilerParams(
            collective_id=cid, has_side_effects=True, vmem_limit_bytes=vmem
        ),
        name=name,
    )


def middle_kernel(
    z, own_h, tok_h, wo_h, wg_h, wu_h, wd_h, wg_o, wu_o, wd_o, seed_h, cot, gain, beta,
    out_part, out_pair, grad_mid, grad_mix, p_wo, p_gate, p_up, p_down, sums,
    send, recv, lsem,
    own, tok, wo, wg, wu, wd, seed, n2, middle, hidden, gg, gu, two, one, rc, ry, tot, out_f,
):
    p, net = Place(z), Net(send, recv, lsem)
    rows, d = z.rows, z.d
    cf = z.cf
    pairs = [(own_h, own), (wo_h, wo), (tok_h, tok)]
    for k in range(z.H):
        h2, lo = (p.h2 + k // 2) % (z.H // 2), (p.lo + k) % 2
        at = part(h2 * 2 + lo, cf)
        if k == 0:
            half = part(p.c, cf)
            pairs += [(wg_o.at[:, half], wg.at[:, at]), (wu_o.at[:, half], wu.at[:, at]),
                      (wd_o.at[half], wd.at[at])]
        else:
            pairs += [(wg_h.at[:, at], wg.at[:, at]), (wu_h.at[:, at], wu.at[:, at]),
                      (wd_h.at[at], wd.at[at])]
    for k, b in enumerate((p.hl * 2 + p.c, p.hl * 2 + 1 - p.c,
                           (1 - p.hl) * 2 + p.c, (1 - p.hl) * 2 + 1 - p.c)):
        at = part(b, rows)
        pairs.append((seed_h.at[at] if k else cot, seed.at[at]))
    loads = [net.local(a, b) for a, b in pairs]
    for cp in loads:
        cp.start()
    meet([p.pair(), p.core()])
    chunk = 128
    blocks = [p.hl * 2 + p.c, p.hl * 2 + 1 - p.c,
              (1 - p.hl) * 2 + 1 - p.c, (1 - p.hl) * 2 + p.c]

    def block_rows(b):
        return pl.ds(pl.multiple_of(b * rows, rows), rows)

    for cp in loads[:3]:
        cp.wait()

    def norm(i, _):
        at = part(i, chunk)
        m = tok[at].astype(F32) + dot(own[at], wo[...])
        middle[at] = m
        scaled, _ = norm_stats(m)
        here = pl.ds(pl.multiple_of(blocks[0] * rows + i * chunk, chunk), chunk)
        n2[here] = (scaled * gain[...] + beta[...]).astype(BF16)
        return 0

    lax.fori_loop(0, rows // chunk, norm, 0)
    mine, far = n2.at[block_rows(blocks[0])], n2.at[block_rows(blocks[3])]
    n_pair, n_core = net.remote(mine, mine, p.pair()), net.remote(mine, mine, p.core())
    n_hop = net.remote(far, far, p.core())
    n_pair.start()
    n_core.start()
    for cp in loads[3:]:
        cp.wait()
    sub = min(256, rows)

    def ffn(b):
        def body(i, _):
            at = pl.ds(pl.multiple_of(b * rows + i * sub, sub), sub)
            a, e = n2[at], seed[at]
            gate, up = dot(a, wg[...]), dot(a, wu[...])
            sig = jax.nn.sigmoid(gate)
            silu = gate * sig
            h = (silu * up).astype(BF16)
            hidden[at] = h
            one[at] = dot(h, wd[...]).astype(BF16)
            gh = dot(e, wd[...], NT)
            g1 = (gh * up * sig * (1.0 + gate * (1.0 - sig))).astype(BF16)
            g2 = (gh * silu).astype(BF16)
            gg[at] = g1
            gu[at] = g2
            two[at] = (dot(g1, wg[...], NT) + dot(g2, wu[...], NT)).astype(BF16)
            return 0

        lax.fori_loop(0, rows // sub, body, 0)

    def send_core(k, b, far):
        ref = (two, one)[k]
        cp = net.remote(ref.at[block_rows(b)], rc.at[k, far], p.core())
        cp.start()
        return cp

    ffn(blocks[0])
    n_core.wait_recv()
    ffn(blocks[1])
    near = [send_core(k, blocks[1], 0) for k in range(2)]
    n_pair.wait_recv()
    n_hop.start()
    n_hop.wait_recv()
    ffn(blocks[2])
    away = [send_core(k, blocks[2], 1) for k in range(2)]
    ffn(blocks[3])
    for k, ref in enumerate((two, one)):
        away[k].wait_recv()
        tot[k] = add_refs(ref[block_rows(blocks[3])], rc[k, 1]).astype(BF16)
        if k == 0:
            to_pair = net.remote(tot.at[0], ry, p.pair())
            to_pair.start()
    stores = []
    for a, b, into, out in ((hidden, seed, wd, p_down), (n2, gg, wg, p_gate), (n2, gu, wu, p_up)):
        for i in range(into.shape[0] // 256):
            at = pl.ds(i * 256, 256)
            into[at] = dot(a[:, at], b[...], TN).astype(BF16)
        stores.append(net.local(into, out))
        stores[-1].start()
    near[0].wait_recv()
    to_pair.wait_recv()

    def back(i, carry):
        at = part(i, chunk)
        here = pl.ds(pl.multiple_of(blocks[0] * rows + i * chunk, chunk), chunk)
        scaled, inverse = norm_stats(middle[at])
        e = add_refs(two[here], rc[0, 0, at], ry[at])
        m = seed[here].astype(F32) + norm_backward(e, scaled, inverse, gain[...])
        out_f[at] = add_refs(middle[at], one[here], rc[1, 0, at])
        middle[at] = m
        tok[at] = m.astype(BF16)
        return (
            carry[0] + jnp.sum(e * scaled, axis=0, keepdims=True),
            carry[1] + jnp.sum(e, axis=0, keepdims=True),
        )

    near[1].wait_recv()
    zero = jnp.zeros((1, d), F32)
    a, b = lax.fori_loop(0, rows // chunk, back, (zero, zero))
    sums[0:1] = a
    sums[1:2] = b
    net.wait_sends()
    for i in range(d // 256):
        at = pl.ds(i * 256, 256)
        n2[at] = dot(own[:, at], tok[...], TN).astype(BF16)
    stores.append(net.local(n2.at[pl.ds(0, d)], p_wo))
    stores.append(net.local(out_f, out_part))
    stores.append(net.local(tot.at[1], out_pair))
    stores.append(net.local(middle, grad_mid))
    for cp in stores[3:]:
        cp.start()
    mixed_at = pl.ds(0, rows)
    two[mixed_at] = dot(tok[...], wo[...], NT).astype(BF16)
    last = net.local(two.at[mixed_at], grad_mix)
    last.start()
    for cp in stores + [last]:
        cp.wait()


def add_refs(*values):
    total = values[0].astype(F32)
    for v in values[1:]:
        total = total + v.astype(F32)
    return total


def lane_of(rows):
    return lax.broadcasted_iota(jnp.int32, (rows, 128), 1)


def rope_tables():
    frequency = np.float32(10000.0) ** (-np.arange(HD // 2, dtype=np.float32) * 2.0 / HD)
    angles = np.arange(WIN, dtype=np.float32)[:, None] * frequency.astype(np.float32)[None, :]
    angles = np.concatenate([angles] * 4, axis=1)
    return np.cos(angles), np.sin(angles)


def turn(v, cosines, sines):
    swapped = jnp.where(
        lane_of(v.shape[0]) % HD < HD // 2, -pltpu.roll(v, 96, 1), pltpu.roll(v, 32, 1)
    )
    return v * cosines + swapped * sines


def spare_lanes(first, v, lane):
    high = v.astype(BF16)
    rest = v - high.astype(F32)
    middle = rest.astype(BF16)
    low = (rest - middle.astype(F32)).astype(BF16)
    s = lane % HD
    tail = jnp.where(s == 2, -middle.astype(F32), jnp.where(s == 3, -low.astype(F32), 0.0))
    return jnp.where(s == 0, first, jnp.where(s == 1, -high.astype(F32), tail))


def run_at(steps, i):
    for at, functions in sorted(steps.items()):

        @pl.when(i == at)
        def _(functions=functions):
            for f in functions:
                f()


def slot_order(p, z):
    half = z.G // 2
    rhi = p.r // 2
    order = [(rhi, p.lo), (rhi, 1 - p.lo)]
    for j in range(1, half):
        order += [((rhi + j) % half, p.lo), ((rhi + j) % half, 1 - p.lo)]
    return [a * 2 + b for a, b in order]


def front_kernel(
    z, n1, w3, cos, sin, bias, wo, wg, wu, wd, cot,
    n1s, w3c, q, k, v, o, qa, own, wos, wgs, wus, wds, seed,
    send, recv, lsem, w3s, mixed,
):
    p, net = Place(z), Net(send, recv, lsem)
    rq, qc = z.d // z.n_dp, z.d // z.n_dp
    rx, dx, cf = z.d // z.X, z.cf // z.X, z.cf
    half, wide = z.G // 2, z.cw % 128 == 0
    rhi = p.r // 2
    hr = z.rows // 2

    def slot_dev(a, b):
        return (p.dp, p.g * z.G + a * 2 + b)

    def slot_rows(a, b, top):
        return pl.ds(pl.multiple_of((a * 2 + b) * z.rows + top * hr, 16), hr)

    near = [((rhi + j) % half) for j in range(1, half)]
    back = [((rhi + half - j) % half) for j in range(1, half)]
    meet(
        [slot_dev(rhi, 1 - p.lo)]
        + [slot_dev(a, 1 - p.lo) for a in near]
        + [p.hdev(i) for i in range(1, z.H)]
        + [p.xdev(i) for i in range(1, z.X)]
        + [p.core()]
    )
    quarter = part(p.dp, rq)
    w_out = [
        net.remote(w3.at[:, quarter], w3s.at[p.g, :, quarter], p.gdev(i)) for i in range(1, z.NG)
    ]
    y_out, a_out = [], []
    for top in (1, 0):
        y_out.append(
            net.remote(n1.at[pl.ds(top * hr, hr)], n1s.at[slot_rows(rhi, p.lo, top)],
                       slot_dev(rhi, 1 - p.lo))
        )
    for top in (0, 1):
        a_out.append(
            [
                net.remote(n1.at[pl.ds(top * hr, hr)], n1s.at[slot_rows(rhi, p.lo, top)],
                           slot_dev(a, p.lo))
                for a in near
            ]
        )
    keep_w = net.local(w3, w3s.at[p.g])
    keep_n = net.local(n1, n1s.at[part(p.r, z.rows)])
    for cp in w_out:
        cp.start()
    y_out[0].start()
    for cp in a_out[0]:
        cp.start()
    keep_w.start()
    keep_n.start()
    y_out[1].start()
    for cp in a_out[1]:
        cp.start()
    for cp in w_out:
        cp.wait_recv()
    w_back = [(p.g + z.NG - i) % z.NG for i in range(1, z.NG)]
    along = []
    for g in w_back:
        block = w3s.at[g, :, quarter]
        along += [net.remote(block, block, p.xdev(i)) for i in range(1, z.X)]
    for cp in along:
        cp.start()
    for cp in along:
        cp.wait_recv()
    across = []
    for g in w_back:
        for x in range(z.X):
            block = w3s.at[g, :, part(x * 2 + p.c, rq)]
            across.append(net.remote(block, block, p.core()))
            across[-1].start()
    y_out[0].wait_recv()
    hop_a = []
    block = n1s.at[slot_rows(rhi, 1 - p.lo, 1)]
    hop_a = [net.remote(block, block, slot_dev(a, p.lo)) for a in near]
    for cp in hop_a:
        cp.start()
    hop_y = []
    for j, a in enumerate(back):
        a_out[0][j].wait_recv()
        block = n1s.at[slot_rows(a, p.lo, 0)]
        hop_y.append(net.remote(block, block, slot_dev(rhi, 1 - p.lo)))
        hop_y[-1].start()
    for cp in across:
        cp.wait_recv()
    keep_w.wait()
    keep_n.wait()
    for m in range(3):
        if wide:
            for g in range(z.NG):
                w3c[m, :, g * z.cw : (g + 1) * z.cw] = w3s[g, m]
        else:
            w3c[m] = add_refs(*[w3s[g, m] for g in range(z.NG)]).astype(BF16)

    def wo_rows(t):
        return part((t % z.G) * z.NG + t // z.G, z.cw)

    cols = part(p.dp, qc)
    own_o = wos.at[wo_rows(p.t), cols]
    o_out = [net.remote(wo.at[:, cols], own_o, p.hdev(i)) for i in range(1, z.H)]
    o_keep = net.local(wo.at[:, cols], own_o)
    o_hop = [net.remote(own_o, own_o, p.y())]
    for i in range(1, z.H):
        block = wos.at[wo_rows(((p.hi + z.H - i) % z.H) * 2 + p.lo), cols]
        o_hop.append(net.remote(block, block, p.y()))
    block = wos.at[:, cols]
    o_along = [net.remote(block, block, p.xdev(i)) for i in range(1, z.X)]
    o_across = []
    for x in range(z.X):
        block = wos.at[:, part(x * 2 + p.c, qc)]
        o_across.append(net.remote(block, block, p.core()))

    def pieces(h2, lo):
        k, x = h2 * 2 + lo, p.x
        return (
            wgs.at[part(x, rx), part(k, cf)],
            wus.at[part(x, rx), part(k, cf)],
            wds.at[pl.ds(pl.multiple_of(k * cf + x * dx, 16), dx)],
        )

    src = (
        wg.at[part(p.x, rx), part(p.c, cf)],
        wu.at[part(p.x, rx), part(p.c, cf)],
        wd.at[pl.ds(pl.multiple_of(p.c * cf + p.x * dx, 16), dx)],
    )
    h2n = z.H // 2
    h2_back = [(p.h2 + h2n - i) % h2n for i in range(1, h2n)]

    def to(refs, device):
        return [net.remote(ref, ref, device) for ref in refs]

    def all_x(refs):
        return [cp for m in range(1, z.X) for cp in to(refs, p.xdev(m))]

    own_piece = pieces(p.h2, p.lo)
    f_z = [[net.remote(a, b, p.h2dev(i)) for a, b in zip(src, own_piece)] for i in range(1, h2n)]
    f_y = [[net.remote(a, b, p.y()) for a, b in zip(src, own_piece)]]
    f_y += [to(pieces(h2, p.lo), p.y()) for h2 in h2_back]
    f_x = [all_x(pieces(p.h2, 1 - p.lo))]
    f_xz = [all_x(pieces(h2, p.lo)) for h2 in h2_back]
    f_x += [all_x(pieces(h2, 1 - p.lo)) for h2 in h2_back]
    mine = seed.at[p.hl * 2 + p.c]
    other = seed.at[(1 - p.hl) * 2 + p.c]
    s_y, s_core = net.remote(cot, mine, p.pair()), net.remote(cot, mine, p.core())
    s_hop = net.remote(other, other, p.core())

    def start(*copies):
        def f():
            for cp in copies:
                cp.start()
        return f

    def arrive(*copies):
        def f():
            for cp in copies:
                cp.wait_recv()
        return f

    width = q.shape[1]
    pairs, bq = width // 128, min(256, z.rows)
    per = z.rows // bq
    blocks = WIN // bq
    total = pairs * blocks
    steps = {}

    def at(i, *functions):
        steps.setdefault(min(i, total - 1), []).extend(functions)

    at(0, arrive(*f_y[0]), start(*f_x[0]))
    at(1, start(s_core, s_y))
    at(2, *[f for i in range(1, z.H) for f in (arrive(o_out[i - 1]), start(o_hop[i]))])
    for m in range(3):
        for i in range(h2n - 1):
            at(3 + m, arrive(f_z[i][m]), start(f_y[i + 1][m], *f_xz[i][m :: 3]))
    at(6, arrive(*o_hop), start(*o_along))
    at(8, arrive(*o_along), start(*o_across))
    for m in range(3):
        for i in range(1, h2n):
            at(9 + m, arrive(f_y[i][m]), start(*f_x[i][m :: 3]))
    at(13, arrive(s_y), start(s_hop))

    order = slot_order(p, z)

    def project(r):
        rows = part(r, z.rows)
        a = n1s[rows]
        for m, ref in enumerate((q, k, v)):
            y = dot(a, w3c[m])
            for j in range(width // 128):
                t = y[:, j * 128 : j * 128 + 128]
                if m < 2:
                    t = turn(t, cos[rows], sin[rows])
                ref[rows, j * 128 : j * 128 + 128] = t.astype(BF16)

    project(order[0])
    y_out[1].wait_recv()
    o_keep.start()
    for group in [o_out] + f_z + f_y[:1]:
        for cp in group:
            cp.start()
    project(order[1])
    o_keep.wait()
    o_hop[0].start()
    for j in range(half - 1):
        a_out[1][j].wait_recv()
        hop_a[j].wait_recv()
        hop_y[j].wait_recv()
    for r in order[2:]:
        project(r)
    lane_k, lane_q = lane_of(WIN), lane_of(bq)

    m_out = {}
    for j in range(pairs):
        for i in range(1, z.G):
            col = pl.ds(pl.multiple_of(p.r * z.hw + j * 128, 128), 128)
            cp = net.remote(
                mixed.at[part(p.ri(i), z.rows), j * 128 : j * 128 + 128],
                own.at[:, col], p.rdev(i),
            )
            m_out[j, i] = cp
            at(j * blocks + i * per - 1, start(cp))

    def block(i, _):
        j, b = i // blocks, i % blocks
        row = ((p.r + 1 + b // per) % z.G) * z.rows + (b % per) * bq
        col, rows = part(j, 128), pl.ds(pl.multiple_of(row, bq), bq)
        k2, v2, kb, q2 = k[:, col], v[:, col], bias[...], q[rows, col]
        mixes = []
        for e in range(2):
            own_k = (lane_k < HD) if e == 0 else (lane_k >= HD)
            own_q = (lane_q < HD) if e == 0 else (lane_q >= HD)
            k_e = jnp.where(own_k, k2, kb)
            v_e = jnp.where(own_k, v2, jnp.ones_like(v2))
            q_e = jnp.where(own_q, q2, jnp.where(lane_q % HD == 0, 1.0, 0.0).astype(BF16))
            s = dot(q_e, k_e, NT)
            top = jnp.max(s, axis=1, keepdims=True)
            prob = jnp.exp2((s - top) * C2).astype(BF16)
            sums = dot(prob, v_e)
            mixes.append(sums / pltpu.roll(sums, HD, 1))
            norm = jnp.where(own_q, 0.0, top + jnp.log2(jnp.where(own_q, 1.0, sums)) * (1.0 / C2))
            full = jnp.where(own_q, q2.astype(F32), spare_lanes(1.0, norm, lane_q))
            qa[2 * j + e, rows] = full.astype(BF16)
        mix = jnp.where(lane_q < HD, mixes[0], mixes[1])
        o[rows, col] = mix
        mixed[rows, col] = mix.astype(BF16)
        run_at(steps, i)
        return 0

    lax.fori_loop(0, total, block, 0)
    m_keep = net.local(mixed.at[part(p.r, z.rows)], own.at[:, part(p.r, z.hw)])
    m_keep.start()
    for cp in list(m_out.values()) + o_across + [s_core, s_hop]:
        cp.wait_recv()
    for group in f_x + f_xz:
        for cp in group:
            cp.wait_recv()
    m_keep.wait()
    net.wait_sends()


def back_kernel(
    z, gm, qa_h, q_h, k_h, v_h, o_h, w3_h, n1_h, dg, du, dd, do_w, out_pair, bias, cos, sin,
    got, out_got, og, ou, od, ow, oo,
    send, recv, lsem,
    qa, q, k, v, o, do, dq, dk, dv, do_e, dk_sum, dv_sum, w3, n1, part_one, p3,
    rgx, rux, rdx, sg, su, sd, rgy, ruy, rdy, rgz, ruz, rdz,
    oc, so, ox, oy, oz, wc, sw, wx, wgr,
):
    p, net = Place(z), Net(send, recv, lsem)
    d, rows = z.d, z.rows
    rq, rx, dx, cf, h2n = d // z.n_dp, d // z.X, z.cf // z.X, z.cf, z.H // 2
    width = q.shape[1]
    bq = min(512, rows)
    per, blocks, pairs = rows // bq, WIN // bq, width // 128
    total = pairs * blocks
    loads = [net.local(a, b) for a, b in (
        (qa_h, qa), (q_h, q), (k_h, k), (v_h, v), (o_h, o),
        (gm.at[:, part(p.r, z.hw)], do.at[part(p.r, rows)]),
    )]
    late = [net.local(a, b) for a, b in (
        (dd.at[:, part(p.x, dx)], sd), (dg.at[part(p.x, rx)], sg), (du.at[part(p.x, rx)], su),
        *[(do_w.at[:, :, part(x * 2 + p.c, rq)], so.at[x]) for x in range(z.X)],
        (w3_h, w3), (n1_h, n1),
    )]
    for cp in loads + late:
        cp.start()
    meet(
        [p.rdev(i) for i in range(1, z.G)]
        + [p.hdev(i) for i in range(1, z.H)]
        + [p.xdev(i) for i in range(1, z.X)]
        + [p.core()]
    )

    def start(*copies):
        def f():
            for cp in copies:
                cp.start()
        return f

    def arrive(*copies):
        def f():
            for cp in copies:
                cp.wait_recv()
        return f

    steps = {}

    def at(i, *functions):
        steps.setdefault(min(i, total - 1), []).extend(functions)

    dest = do.at[part(p.r, rows)]
    a_out = [net.remote(gm.at[:, part(p.ri(i), z.hw)], dest, p.rdev(i)) for i in range(1, z.G)]
    for cp in a_out:
        cp.start()
    def spot(h2, lo):
        return h2 * 2 + lo

    bufs = ((dd, rdx, sd, rdy, rdz, od), (dg, rgx, sg, rgy, rgz, og), (du, rux, su, ruy, ruz, ou))

    def rows_of(m, ref, x):
        return ref.at[:, part(x, dx)] if m == 0 else ref.at[part(x, rx)]

    def piece(m, ref, s):
        return ref.at[s] if m == 0 else ref.at[:, part(s, cf)]

    fx = [[net.remote(rows_of(m, bufs[m][0], p.xi(i)), bufs[m][1].at[i - 1], p.xdev(i))
           for i in range(1, z.X)] for m in range(3)]
    fy = [[net.remote(piece(m, bufs[m][2], spot(h2, 1 - p.lo)), bufs[m][3].at[h2], p.y())
           for h2 in range(h2n)] for m in range(3)]
    fz = [[net.remote(piece(m, bufs[m][2], spot((p.h2 + i) % h2n, p.lo)), bufs[m][4].at[i - 1],
                      p.h2dev(i)) for i in range(1, h2n)] for m in range(3)]
    done_at = [
        (pl.ds(pl.multiple_of(p.c * cf + p.x * dx, 16), dx),),
        (part(p.x, rx), part(p.c, cf)),
        (part(p.x, rx), part(p.c, cf)),
    ]
    fa, fc = [], []
    for m in range(3):
        block = bufs[m][5].at[done_at[m]]
        fa.append([net.remote(block, block, p.xdev(i)) for i in range(1, z.X)])
        block = od.at[part(p.c, cf)] if m == 0 else bufs[m][5].at[:, part(p.c, cf)]
        fc.append(net.remote(block, block, p.core()))

    def ffn_x(m):
        def f():
            arrive(*fx[m])()
            late[m].wait()
            got_x, own = bufs[m][1], bufs[m][2]
            for h in range(2 * h2n):
                if m == 0:
                    own[h] = add_refs(own[h], *[got_x[i, h] for i in range(z.X - 1)]).astype(BF16)
                else:
                    c = pl.ds(h * cf, cf)
                    own[:, c] = add_refs(
                        own[:, c], *[got_x[i, :, c] for i in range(z.X - 1)]
                    ).astype(BF16)
            start(*fy[m])()
        return f

    def ffn_y(m):
        def f():
            arrive(*fy[m])()
            own, got_y = bufs[m][2], bufs[m][3]
            for h2 in range(h2n):
                if m == 0:
                    own[spot(h2, p.lo)] = add_refs(own[spot(h2, p.lo)], got_y[h2]).astype(BF16)
                else:
                    c = part(spot(h2, p.lo), cf)
                    own[:, c] = add_refs(own[:, c], got_y[h2]).astype(BF16)
            start(*fz[m])()
        return f

    def ffn_z(m):
        def f():
            arrive(*fz[m])()
            own, got_z, out = bufs[m][2], bufs[m][4], bufs[m][5]
            s = spot(p.h2, p.lo)
            mine = own[s] if m == 0 else own[:, part(s, cf)]
            out[done_at[m]] = add_refs(mine, *[got_z[i] for i in range(h2n - 1)]).astype(BF16)
            start(*fa[m])()
        return f

    def ffn_c(m):
        def f():
            arrive(*fa[m])()
            fc[m].start()
        return f

    half = z.G // 2
    c_out = [net.remote(do_w.at[:, :, part(p.xi(i) * 2 + 1 - p.c, rq)], oc.at[i], p.core())
             for i in range(z.X)]
    c_x = [net.remote(so.at[p.xi(i)], ox.at[i - 1], p.xdev(i)) for i in range(1, z.X)]
    c_y = [net.remote(so.at[p.x, i * 2 + 1 - p.lo], oy.at[i], p.y()) for i in range(half)]
    c_z = [net.remote(so.at[p.x, (p.hii(i) % half) * 2 + p.lo, part(p.hii(i) // half, z.cw)],
                      oz.at[i - 1], p.hdev(i)) for i in range(1, z.H)]
    cols = part(p.dp, rq)
    block = oo.at[:, cols]
    c_a = [net.remote(block, block, p.xdev(i)) for i in range(1, z.X)]
    c_c = []
    for x in range(z.X):
        block = oo.at[:, part(x * 2 + p.c, rq)]
        c_c.append(net.remote(block, block, p.core()))

    def wo_c():
        for cp in late[3 : 3 + z.X]:
            cp.wait()
        for i in list(range(1, z.X)) + [0]:
            c_out[i].wait_recv()
            for r in range(z.G):
                so[p.xi(i), r] = add_refs(so[p.xi(i), r], oc[i, r]).astype(BF16)
        start(*c_x)()

    def wo_x():
        arrive(*c_x)()
        for r in range(z.G):
            so[p.x, r] = add_refs(so[p.x, r], *[ox[i, r] for i in range(z.X - 1)]).astype(BF16)
        start(*c_y)()

    def wo_y():
        arrive(*c_y)()
        for i in range(half):
            r = i * 2 + p.lo
            so[p.x, r] = add_refs(so[p.x, r], oy[i]).astype(BF16)
        start(*c_z)()

    def wo_z():
        arrive(*c_z)()
        mine = so[p.x, (p.hi % half) * 2 + p.lo, part(p.hi // half, z.cw)]
        oo[:, cols] = add_refs(mine, *[oz[i] for i in range(z.H - 1)]).astype(BF16)
        start(*c_a)()

    def wo_a():
        arrive(*c_a)()
        start(*c_c)()

    o_send = net.remote(out_pair, out_got, p.pair())
    start(*fx[0], *c_out)()
    at(0, wo_c, start(*fx[1]))
    at(1, start(o_send))
    at(2, ffn_x(0), wo_x)
    at(3, start(*fx[2]))
    at(4, ffn_y(0), wo_y)
    at(5, ffn_x(1), wo_z)
    at(6, ffn_z(0), wo_a)
    at(7, ffn_y(1), ffn_c(0))

    for cp in loads:
        cp.wait()
    lane_q, sub = lane_of(bq), 1024
    lane_k = lane_of(sub)
    s64 = lane_k % HD
    ones3 = jnp.where((s64 >= 1) & (s64 <= 3), 1.0, 0.0).astype(BF16)

    def block_step(i, _):
        j, b = i // blocks, i % blocks
        for n in range(1, z.G):

            @pl.when((j == 0) & (b == n * per))
            def _():
                a_out[z.G - 1 - n].wait_recv()

        row = ((p.r + b // per) % z.G) * rows + (b % per) * bq
        col, at_q = part(j, 128), pl.ds(pl.multiple_of(row, bq), bq)
        q2, do2 = q[at_q, col], do[at_q, col]
        prod = do2.astype(F32) * o[at_q, col]
        for e in range(2):
            own_q = (lane_q < HD) if e == 0 else (lane_q >= HD)
            delta = jnp.sum(jnp.where(own_q, prod, 0.0), axis=1, keepdims=True)
            spare = spare_lanes(0.0, jnp.broadcast_to(delta, prod.shape), lane_q)
            do_e[e] = jnp.where(own_q, do2.astype(F32), spare).astype(BF16)
        dqs = [jnp.zeros((bq, 128), F32)] * 2
        for s in range(WIN // sub):
            keys = pl.ds(s * sub, sub)
            k2, v2 = k[keys, col], v[keys, col]
            kb = bias[keys] + ones3
            dks, dvs = [], []
            for e in range(2):
                own_k = (lane_k < HD) if e == 0 else (lane_k >= HD)
                k_e = jnp.where(own_k, k2, kb)
                v_e = jnp.where(own_k, v2, ones3)
                prob = jnp.exp2(dot(k_e, qa[2 * j + e, at_q], NT) * C2)
                ds = (prob * dot(v_e, do_e[e], NT)).astype(BF16)
                dvs.append(dot(prob.astype(BF16), do2))
                dks.append(dot(ds, q2))
                dqs[e] = dqs[e] + dot(ds, k2, TN)
            dv_new = jnp.where(lane_k < HD, dvs[0], dvs[1])
            dk_new = jnp.where(lane_k < HD, dks[0], dks[1])

            @pl.when(b == 0)
            def _():
                dv_sum[keys] = dv_new
                dk_sum[keys] = dk_new

            @pl.when(b > 0)
            def _():
                dv_sum[keys] += dv_new
                dk_sum[keys] += dk_new

        dq_new = jnp.where(lane_q < HD, dqs[0], dqs[1]) * SCALE
        dq[at_q, col] = turn(dq_new, cos[at_q], -sin[at_q]).astype(BF16)

        @pl.when(b == blocks - 1)
        def _():
            dv[:, col] = dv_sum[...].astype(BF16)
            dk[:, col] = turn(dk_sum[...] * SCALE, cos[...], -sin[...]).astype(BF16)

        run_at(steps, i)
        return 0

    lax.fori_loop(0, total, block_step, 0)

    for cp in late[3 + z.X :]:
        cp.wait()
    r_out = []
    for i in list(range(1, z.G)) + [0]:
        here = part(p.ri(i), rows)
        part_one[here] = (
            dot(dq[here], w3[0], NT) + dot(dk[here], w3[1], NT) + dot(dv[here], w3[2], NT)
        ).astype(BF16)
        if i:
            r_out.append(net.remote(part_one.at[here], got.at[i - 1], p.rdev(i)))
            r_out[-1].start()
    r_keep = net.local(part_one.at[part(p.r, rows)], got.at[z.G - 1])
    r_keep.start()
    for m, t in enumerate((dq, dk, dv)):
        y = dot(n1[...], t[...], TN).astype(BF16)
        for g in range(z.NG):
            p3[g, m] = y[:, g * z.cw : (g + 1) * z.cw]
    w_c = [net.remote(p3.at[:, :, part(p.xi(i) * 2 + 1 - p.c, rq)], wc.at[i], p.core())
           for i in range(z.X)]
    start(*w_c)()
    ffn_x(2)()
    w_x = []
    for i in list(range(1, z.X)) + [0]:
        w_c[i].wait_recv()
        for g in range(z.NG):
            sw[i, g] = add_refs(p3[g, :, part(p.xi(i) * 2 + p.c, rq)], wc[i, g]).astype(BF16)
        if i:
            w_x.append(net.remote(sw.at[i], wx.at[i - 1], p.xdev(i)))
            w_x[-1].start()
    ffn_z(1)()
    arrive(*w_x)()
    for g in range(z.NG):
        sw[0, g] = add_refs(sw[0, g], *[wx[i, g] for i in range(z.X - 1)]).astype(BF16)
    w_g = [net.remote(sw.at[0, p.gi(i)], wgr.at[i - 1], p.gdev(i)) for i in range(1, z.NG)]
    start(*w_g)()
    ffn_y(2)()
    ffn_c(1)()
    arrive(*w_g)()
    quarter = part(p.dp, rq)
    for m in range(3):
        ow[m, quarter] = add_refs(
            sw[0, p.g, m], *[wgr[i, m] for i in range(z.NG - 1)]
        ).astype(BF16)
    block = ow.at[:, quarter]
    w_a = [net.remote(block, block, p.xdev(i)) for i in range(1, z.X)]
    start(*w_a)()
    ffn_z(2)()
    arrive(*w_a)()
    w_last = []
    for x in range(z.X):
        block = ow.at[:, part(x * 2 + p.c, rq)]
        w_last.append(net.remote(block, block, p.core()))
        w_last[-1].start()
    ffn_c(2)()
    arrive(*c_c, *fc, *w_last, o_send, *r_out)()
    r_keep.wait()
    net.wait_sends()


def sum_norms_kernel(z, own, out, send, recv, lsem, far, near):
    p, net = Place(z), Net(send, recv, lsem)
    t_dev = [(p.dp, (p.t + i) % z.n_t) for i in range(1, z.n_t)]
    d_dev = [((p.dp + i) % z.n_dp, p.t) for i in range(1, z.n_dp)]
    meet(t_dev + d_dev)
    first = [net.remote(own, far.at[p.t], dev) for dev in t_dev]
    for cp in first:
        cp.start()
    far[p.t] = own[...]
    for cp in first:
        cp.wait_recv()
    near[p.dp] = add_refs(*[far[i] for i in range(z.n_t)])
    second = [net.remote(near.at[p.dp], near.at[p.dp], dev) for dev in d_dev]
    for cp in second:
        cp.start()
    for cp in second:
        cp.wait_recv()
    out[...] = add_refs(*[near[i] for i in range(z.n_dp)])
    net.wait_sends()


def norm_stats(v):
    centre = v - jnp.mean(v, axis=-1, keepdims=True)
    inverse = lax.rsqrt(jnp.mean(centre * centre, axis=-1, keepdims=True) + EPSILON)
    return centre * inverse, inverse


def norm_backward(grad_in, scaled, inverse, gain):
    weighted = grad_in * gain
    first_mean = jnp.mean(weighted, axis=-1, keepdims=True)
    second_mean = jnp.mean(weighted * scaled, axis=-1, keepdims=True)
    return inverse * (weighted - first_mean - scaled * second_mean)


def per_device(
    n_dp, n_t, tokens, lengths, ln1_gain, ln1_bias, w_query, w_key, w_value, w_out,
    ln2_gain, ln2_bias, w_gate, w_up, w_down, cotangent,
):
    rows, d = tokens.shape
    cw, cfull = w_query.shape[1], w_gate.shape[1]
    z = Sizes(n_dp, n_t, rows, d, cw, cfull)
    G, NG, H, X, hw, cf = z.G, z.NG, z.H, z.X, z.hw, z.cf
    rq, rx, dx = d // n_dp, d // X, cf // X
    slot = lax.axis_index("tensor") // G
    length = lax.dynamic_index_in_dim(lengths, slot, keepdims=False)
    lane = lax.broadcasted_iota(jnp.int32, (WIN, 128), 1) % HD
    place = lax.broadcasted_iota(jnp.int32, (WIN, 128), 0)
    bias = jnp.where((lane == 0) & (place >= length), -1e30, 0.0).astype(BF16)
    cos, sin = (jnp.asarray(t, F32) for t in rope_tables())

    own_tokens = tokens.astype(F32)
    scaled_one, inverse_one = norm_stats(own_tokens)
    normed_one = (scaled_one * ln1_gain + ln1_bias).astype(BF16)
    w_three = jnp.stack([w_query, w_key, w_value])
    if cw % 128:
        wider = jnp.zeros((3, d, hw), BF16)
        w_three = lax.dynamic_update_slice(wider, w_three, (0, 0, slot * cw))
    n1, w3, q, k, v, o, qa, mixed_own, wo, wg, wu, wd, seed = comm_call(
        front_kernel, z, "front", 1,
        (
            shape((WIN, d)), shape((3, d, hw)), shape((WIN, hw)), shape((WIN, hw)),
            shape((WIN, hw)), shape((WIN, hw), F32), shape((hw // HD, WIN, 128)),
            shape((rows, d)), shape((d, d)), shape((d, H * cf)), shape((d, H * cf)),
            shape((H * cf, d)), shape((4, rows, d)),
        ),
        [HBM, HBM, VMEM, VMEM, VMEM] + [HBM] * 5,
        [VMEM] * 9 + [HBM] * 4,
        [pltpu.VMEM((NG,) + w_three.shape, BF16), pltpu.VMEM((WIN, hw), BF16)],
        n=160, vmem=60 * MIB,
    )(normed_one, w_three, cos, sin, bias, w_out, w_gate, w_up, w_down, cotangent)
    every = 4 * rows
    width = H * cf
    mid_out = (
        shape((rows, d), F32), shape((rows, d)), shape((rows, d), F32), shape((rows, d)),
        shape((d, d)), shape((d, width)), shape((d, width)), shape((width, d)), shape((2, d), F32),
    )
    out_part, out_pair, grad_middle, grad_mixed, p_wo, p_gate, p_up, p_down, sums_two = comm_call(
        middle_kernel, z, "middle", 4, mid_out,
        [HBM] * 11 + [VMEM] * 2, [HBM] * 8 + [VMEM],
        [
            pltpu.VMEM((rows, d), BF16), pltpu.VMEM((rows, d), BF16), pltpu.VMEM((d, d), BF16),
            pltpu.VMEM((d, width), BF16), pltpu.VMEM((d, width), BF16),
            pltpu.VMEM((width, d), BF16), pltpu.VMEM((every, d), BF16),
            pltpu.VMEM((every, d), BF16), pltpu.VMEM((rows, d), F32),
            pltpu.VMEM((every, width), BF16), pltpu.VMEM((every, width), BF16),
            pltpu.VMEM((every, width), BF16), pltpu.VMEM((every, d), BF16),
            pltpu.VMEM((every, d), BF16), pltpu.VMEM((2, 2, rows, d), BF16),
            pltpu.VMEM((rows, d), BF16), pltpu.VMEM((2, rows, d), BF16),
            pltpu.VMEM((rows, d), F32),
        ],
        vmem=60 * MIB,
    )(
        mixed_own, tokens, wo, wg, wu, wd, w_gate, w_up, w_down, seed.reshape(every, d), cotangent,
        ln2_gain.reshape(1, d), ln2_bias.reshape(1, d),
    )
    gain_two, bias_two = sums_two[0], sums_two[1]
    p_wo = p_wo.reshape(G, hw, d)
    p_down = p_down.reshape(H, cf, d)
    V = pltpu.VMEM
    pieces = ((rx, cf), (rx, cf), (dx, d))
    got, out_got, g_gate, g_up, g_down, g_w3, g_wo = comm_call(
        back_kernel, z, "back", 8,
        (
            shape((G, rows, d)), shape((rows, d)), shape((d, 2 * cf)), shape((d, 2 * cf)),
            shape((2 * cf, d)), shape((3, d, cw)), shape((cw, d)),
        ),
        [HBM] * 13 + [VMEM] * 3, [HBM] * 2 + [VMEM] * 5,
        [
            V((hw // HD, WIN, 128), BF16), V((WIN, hw), BF16), V((WIN, hw), BF16),
            V((WIN, hw), BF16), V((WIN, hw), F32), V((WIN, hw), BF16), V((WIN, hw), BF16),
            V((WIN, hw), BF16), V((WIN, hw), BF16), V((2, min(512, rows), 128), BF16),
            V((WIN, 128), F32), V((WIN, 128), F32), V((3, d, hw), BF16), V((WIN, d), BF16),
            V((WIN, d), BF16), V((NG, 3, d, cw), BF16),
            V((X - 1, rx, width), BF16), V((X - 1, rx, width), BF16), V((X - 1, H, dx, d), BF16),
            V((rx, width), BF16), V((rx, width), BF16), V((H, dx, d), BF16),
            *[V((H // 2,) + dims, BF16) for dims in pieces],
            *[V((H // 2 - 1,) + dims, BF16) for dims in pieces],
            V((X, G, hw, rq), BF16), V((X, G, hw, rq), BF16), V((X - 1, G, hw, rq), BF16),
            V((G // 2, hw, rq), BF16), V((H - 1, cw, rq), BF16),
            V((X, NG, 3, rq, cw), BF16), V((X, NG, 3, rq, cw), BF16),
            V((X - 1, NG, 3, rq, cw), BF16), V((NG - 1, 3, rq, cw), BF16),
        ],
        n=160, vmem=62 * MIB,
    )(
        grad_mixed, qa, q, k, v, o, w3, n1, p_gate, p_up, p_down, p_wo, out_pair, bias, cos, sin,
    )
    output = (out_part + out_got.astype(F32)).astype(BF16)
    grad_one = jnp.sum(got.astype(F32), axis=0)
    gain_one = jnp.sum(grad_one * scaled_one, axis=0)
    bias_one = jnp.sum(grad_one, axis=0)
    back_one = norm_backward(grad_one, scaled_one, inverse_one, ln1_gain)
    grad_tokens = (grad_middle + back_one).astype(BF16)
    norms = comm_call(
        sum_norms_kernel, z, "sum_norms", 9, shape((4, d), F32), [VMEM], VMEM,
        [V((n_t, 4, d), F32), V((n_dp, 4, d), F32)],
    )(jnp.stack([gain_one, bias_one, gain_two, bias_two]))
    return (
        output, grad_tokens, norms[0], norms[1],
        g_w3[0].astype(F32), g_w3[1].astype(F32), g_w3[2].astype(F32), g_wo.astype(F32),
        norms[2], norms[3], g_gate.astype(F32), g_up.astype(F32), g_down.astype(F32),
    )


def solution(mesh):
    rows, cols, each = P(("dp", "tensor"), None), P(None, "tensor"), P("tensor", None)
    return jax.shard_map(
        functools.partial(per_device, mesh.shape["dp"], mesh.shape["tensor"]),
        mesh=mesh,
        in_specs=(
            rows, P("dp"), P(), P(), cols, cols, cols, each, P(), P(), cols, cols, each, rows,
        ),
        out_specs=(
            rows, rows, P(), P(), cols, cols, cols, each, P(), P(), cols, cols, each,
        ),
        check_vma=False,
    )
```

time: 1990 us -> 449 us (0.23)
  waiting for transfers between devices: 1020 us -> 0 us
  matrix products: 511 us -> 0 us
  Pallas kernels: 0 us -> 416 us
  local copies, waits for them, and re-layouts: 210 us -> 3 us
  other arithmetic: 162 us -> 23.9 us
  blocking collectives: 39.4 us -> 0 us
    psum x3 -> x0, waiting for transfers between devices: 527 us -> none  [the longest x1 268 us: per_device(): lax.psum(jnp.dot(mixed_low, w_out, preferred_element_type=jnp.float32).as...]
    dot_general x77 -> x0, matrix products: 511 us -> none  [the longest x8 131 us: one_one_block(): jnp.einsum('hqk,khd->qhd', grad_scores, key_slot, preferred_element_type=...]
    pallas_call x0 -> x4, Pallas kernels: none -> 416 us  [the longest x1 188 us: per_device(): comm_call(back_kernel, z, 'back', 8, (shape((G, rows, d)), shape((rows, d...]
    reduce_scatter x2 -> x0, waiting for transfers between devices: 287 us -> none  [the longest x1 148 us: per_device(): lax.psum_scatter((summed + lax.dot_general(grad_values, w_value, LAST_DIM...]
    all_gather x2 -> x0, waiting for transfers between devices: 202 us -> none  [the longest x1 121 us: per_device(): lax.all_gather(tokens, 'tensor', axis=0, tiled=True).astype(jnp.float32)]
    dynamic_update_slice x10 -> x0, local copies, waits for them, and re-layouts: 89.2 us -> none  [attend_backward(): lax.map(one_slot, (queries.reshape(block_shape), grad_mixed.reshape(block...]
    convert_element_type x15 -> x9, other arithmetic: 61 us -> 15.9 us  [the longest x1 3.29 us: per_device(): grad_tokens = (grad_middle + back_one).astype(BF16)]
    while x66 -> x0, local copies, waits for them, and re-layouts: 39.9 us -> none
  transfers between devices with their start and end apart: 7 -> 0, of which waited for: 7 -> 0; matrix products, arithmetic and copies ran while one was open for 8% -> 0% of each run, Pallas kernels for 0% -> 0%
where the time goes in v2:
time: 449 us; the launch traced here: 444 us
  Pallas kernels  416 us (93%)
  other arithmetic  23.9 us (5%)
    pallas_call x1, Pallas kernels, per_device(): comm_call(back_kernel, z, 'back', 8, (shape((G, rows, d)), shape((rows, d...  188 us
    pallas_call x1, Pallas kernels, per_device(): comm_call(front_kernel, z, 'front', 1, (shape((WIN, d)), shape((3, d, hw)...  140 us
    pallas_call x1, Pallas kernels, per_device(): comm_call(middle_kernel, z, 'middle', 4, mid_out, [HBM] * 11 + [VMEM] * 2...  76.4 us
    pallas_call x1, Pallas kernels, per_device(): comm_call(sum_norms_kernel, z, 'sum_norms', 9, shape((4, d), F32), [VMEM]...  11.8 us

profile of v2, /device:TPU:0, one launch (start us, length us, event | category | flops | bytes accessed | tf_op | source)
XLA Modules:
  0.0 443.9 jit_solution(3713975751686915358)
XLA Ops:
  0.7 1.3 dynamic_slice.4
  2.0 0.7 iota_compare_fusion
  2.7 0.0 copy-start.13
  2.7 1.5 convert_reduce_fusion.2
  4.2 1.6 fusion.14
  5.9 1.1 select_convert_fusion.bias
  7.0 1.0 pad_maximum_fusion.w3
  8.0 1.4 fusion.7.n1
  9.4 139.6 %front.1 = (bf16[2048,1024]{1,0:T(8,128)(2,1)}, bf16[3,1024,256]{2,1,0:T(8,128)(2,1)}, bf16[2048,256]{1,0:T(8,128)(2,1)}, bf16[2048,256]{1,0:T(8,128)(2,1)}, bf1...) custom-call(bf16[512,1024]{1,0:T(8,128)(2,1)} %fusion.7.n1, ...), custom_call_target="tpu_custom_call" | custom-call | tf_op jit(solution)/shard_map/front/pallas_call | solution.py:978
  149.0 76.4 %middle.1 = (f32[512,1024]{1,0:T(8,128)}, bf16[512,1024]{1,0:T(8,128)(2,1)}, f32[512,1024]{1,0:T(8,128)}, bf16[512,1024]{1,0:T(8,128)(2,1)}, bf16[1024,1024]{1,0...) custom-call(bf16[512,1024]{1,0:T(8,128)(2,1)} %get-tuple-element.42., ...), custom_call_target="tpu_custom_call" | custom-call | tf_op jit(solution)/shard_map/middle/pallas_call | solution.py:997
  225.4 188.2 %back.1 = (bf16[4,512,1024]{2,1,0:T(8,128)(2,1)}, bf16[512,1024]{1,0:T(8,128)(2,1)}, bf16[1024,512]{1,0:T(8,128)(2,1)}, bf16[1024,512]{1,0:T(8,128)(2,1)}, bf16[...) custom-call(bf16[512,1024]{1,0:T(8,128)(2,1)} %get-tuple-element.49.gm, ...), custom_call_target="tpu_custom_call" | custom-call | tf_op jit(solution)/shard_map/back/pallas_call | solution.py:1021
  413.6 3.3 add_convert_fusion
  416.9 0.8 convert_element_type.64
  417.7 1.2 bitcast_convert_fusion
  418.9 1.6 convert_element_type.65
  420.5 1.6 convert_element_type.66
  422.1 1.6 convert_element_type.67
  423.7 0.1 copy-done.2
  423.8 1.7 convert_reduce_fusion
  425.6 0.9 fusion.13
  426.5 0.6 pad_maximum_fusion.1.own
  427.1 11.8 %sum_norms.1 = f32[4,1024]{1,0:T(4,128)} custom-call(f32[4,1024]{1,0:T(4,128)} %pad_maximum_fusion.1.own), custom_call_target="tpu_custom_call" | custom-call | tf_op jit(solution)/shard_map/sum_norms/pallas_call | solution.py:1053
  438.9 1.5 fusion.16
  440.4 3.3 fusion.12
  (32 shorter events, 0.1 us)
Async XLA Ops:
  0.6 6.4 %copy-start.8 = (bf16[1024,128]{1,0:T(8,128)(2,1)S(1)}, bf16[1024,128]{1,0:T(8,128)(2,1)}, u32[]{:S(2)}) copy-start(bf16[1024,128]{1,0:T(8,128)(2,1)} %param.22) | copy-start | bytes 786436
  0.7 6.4 %copy-start.9 = (bf16[1024,128]{1,0:T(8,128)(2,1)S(1)}, bf16[1024,128]{1,0:T(8,128)(2,1)}, u32[]{:S(2)}) copy-start(bf16[1024,128]{1,0:T(8,128)(2,1)} %param.21) | copy-start | bytes 786436
  0.7 6.4 %copy-start.10 = (bf16[1024,128]{1,0:T(8,128)(2,1)S(1)}, bf16[1024,128]{1,0:T(8,128)(2,1)}, u32[]{:S(2)}) copy-start(bf16[1024,128]{1,0:T(8,128)(2,1)} %param.20) | copy-start | bytes 786436
  2.7 5.3 %copy-start = (bf16[512,1024]{1,0:T(8,128)(2,1)S(1)}, bf16[512,1024]{1,0:T(8,128)(2,1)}, u32[]{:S(2)}) copy-start(bf16[512,1024]{1,0:T(8,128)(2,1)} %tok_h.1) | copy-start | bytes 3145732
  2.7 5.3 %copy-start.11 = (f32[1024]{0:T(1024)S(1)}, f32[1024]{0:T(1024)}, u32[]{:S(2)}) copy-start(f32[1024]{0:T(1024)} %param.18) | copy-start | bytes 12292
  2.7 5.3 %copy-start.13 = (f32[1024]{0:T(1024)S(1)}, f32[1024]{0:T(1024)}, u32[]{:S(2)}) copy-start(f32[1024]{0:T(1024)} %param.19) | copy-start | bytes 12292
  413.6 3.3 copy-start.7
  413.6 4.1 copy-start.6
  416.9 2.0 copy-start.5
  418.9 1.6 copy-start.4
  418.9 3.2 copy-start.3
  420.5 3.3 copy-start.2
  423.8 1.7 copy-start.1
  425.6 0.9 copy-start.12
